TPU v7x, 32 devices: a whole 2x2x4 slice. The times are simulated.
32 devices in a mesh: dp: 8 (over y, x, core), tensor: 4 (over z).
Axes of the slice: x: 2, y: 2, z: 4, core: 2. Of those that a mesh axis runs over, the one named last changes fastest.
Arguments:
- tokens: bfloat16 [16, 1024, 768], P('dp', 'tensor'), may hold values from -6 to 6
- segment_ids: int32 [16, 1024], P('dp'), may hold values from 0 to 1023, as said below
- gain_first: float32 [768], replicated, may hold values from 0.5 to 1.5
- shift_first: float32 [768], replicated, may hold values from -3 to 3
- weight_qkv: bfloat16 [768, 3, 768], P(None, None, 'tensor'), may hold values from -0.21875 to 0.21875
- bias_qv: float32 [2, 768], P(None, 'tensor'), may hold values from -3 to 3
- weight_out: bfloat16 [768, 768], P('tensor'), may hold values from -0.625 to 0.625
- bias_out: float32 [768], replicated, may hold values from -3 to 3
- gain_second: float32 [768], replicated, may hold values from 0.5 to 1.5
- shift_second: float32 [768], replicated, may hold values from -3 to 3
- weight_up: bfloat16 [768, 3072], P(None, 'tensor'), may hold values from -0.21875 to 0.21875
- bias_up: float32 [3072], P('tensor'), may hold values from -3 to 3
- weight_down: bfloat16 [3072, 768], P('tensor'), may hold values from -0.15625 to 0.15625
- bias_down: float32 [768], replicated, may hold values from -3 to 3
- cotangent: bfloat16 [16, 1024, 768], P('dp', 'tensor'), may hold values from -6 to 6
Outputs:
- block_out: bfloat16 [16, 1024, 768], P('dp', 'tensor')
- input_grad: float32 [16, 1024, 768], P('dp', 'tensor')
- gain_first_grad: float32 [768], replicated
- shift_first_grad: float32 [768], replicated
- weight_qkv_grad: float32 [768, 3, 768], P(None, None, 'tensor')
- bias_qv_grad: float32 [2, 768], P(None, 'tensor')
- weight_out_grad: float32 [768, 768], P('tensor')
- bias_out_grad: float32 [768], replicated
- gain_second_grad: float32 [768], replicated
- shift_second_grad: float32 [768], replicated
- weight_up_grad: float32 [768, 3072], P(None, 'tensor')
- bias_up_grad: float32 [3072], P('tensor')
- weight_down_grad: float32 [3072, 768], P('tensor')
- bias_down_grad: float32 [768], replicated
Inputs may be any that keep to these rules, and one draw needn't show every extreme that they name: `segment_ids`: along each row the ids start at 0, never fall, and rise by at most one from one position to the next. In each aligned block of 2 rows one row is a single cell, and in some row every position is a cell of its own.
All inputs are finite; a program needn't handle non-finite values.
Results may differ from a plain program's by a relative error of at most 0.018.
Values may be sent and summed in bfloat16 or wider, within the bound.
A program may use at most 128 MiB of HBM per device.

v0:
```python
import jax
import jax.numpy as jnp
from jax import lax
from jax.sharding import PartitionSpec as P

HEAD = 64


def layer_norm(inputs, scaling, offset):
    center = inputs - jnp.mean(inputs, axis=-1, keepdims=True)
    spread = jnp.mean(center * center, axis=-1, keepdims=True)
    return center * lax.rsqrt(spread + 1e-05) * scaling + offset


def exact_gelu(values):
    return jax.nn.gelu(values, approximate=False)


def contract_rows(left, right):
    return lax.dot_general(
        left, right, (((0,), (0,)), ((), ())), preferred_element_type=jnp.float32
    )


def contract_cols(left, right):
    return lax.dot_general(
        left, right, (((1,), (1,)), ((), ())), preferred_element_type=jnp.float32
    )


def body(
    tokens,
    segment_ids,
    gain_first,
    shift_first,
    weight_qkv,
    bias_qv,
    weight_out,
    bias_out,
    gain_second,
    shift_second,
    weight_up,
    bias_up,
    weight_down,
    bias_down,
    cotangent,
):
    micro_count, share_rows, model_width = tokens.shape
    length = segment_ids.shape[1]
    local_width = weight_qkv.shape[2]
    local_heads = local_width // HEAD
    local_hidden = weight_up.shape[1]
    scale = HEAD ** (-0.5)
    qkv_flat = weight_qkv.reshape(model_width, 3 * local_width)

    def attend(queries, keys_low, id_row):
        raw_scores = (
            jnp.einsum("qhd,khd->hqk", queries, keys_low, preferred_element_type=jnp.float32)
            * scale
        )
        same_cell = id_row[:, None] == id_row[None, :]
        return jnp.where(same_cell[None], raw_scores, -1e30)

    def run_forward(x_row, id_row):
        inputs = x_row.astype(jnp.float32)
        normed = layer_norm(inputs, gain_first, shift_first).astype(jnp.bfloat16)
        sent_first = lax.all_gather(normed, "tensor", axis=0, tiled=True)
        projected = jnp.dot(sent_first, qkv_flat, preferred_element_type=jnp.float32)
        projected = projected.reshape(length, 3, local_width)
        queries = (
            (projected[:, 0] + bias_qv[0]).astype(jnp.bfloat16).reshape(length, local_heads, HEAD)
        )
        keys_low = projected[:, 1].astype(jnp.bfloat16).reshape(length, local_heads, HEAD)
        values_low = (
            (projected[:, 2] + bias_qv[1]).astype(jnp.bfloat16).reshape(length, local_heads, HEAD)
        )
        scores = attend(queries, keys_low, id_row)
        log_totals = jax.nn.logsumexp(scores, axis=-1, keepdims=True)
        weights_low = jnp.exp(scores - log_totals).astype(jnp.bfloat16)
        context = jnp.einsum(
            "hqk,khd->qhd", weights_low, values_low, preferred_element_type=jnp.float32
        )
        context = context.reshape(length, local_width).astype(jnp.bfloat16)
        attended = lax.psum_scatter(
            jnp.dot(context, weight_out, preferred_element_type=jnp.float32).astype(jnp.bfloat16),
            "tensor",
            scatter_dimension=0,
            tiled=True,
        ).astype(jnp.float32)
        middle = inputs + attended + bias_out
        normed_second = layer_norm(middle, gain_second, shift_second).astype(jnp.bfloat16)
        sent_second = lax.all_gather(normed_second, "tensor", axis=0, tiled=True)
        hidden_pre = jnp.dot(sent_second, weight_up, preferred_element_type=jnp.float32) + bias_up
        active = exact_gelu(hidden_pre).astype(jnp.bfloat16)
        fed_forward = lax.psum_scatter(
            jnp.dot(active, weight_down, preferred_element_type=jnp.float32).astype(jnp.bfloat16),
            "tensor",
            scatter_dimension=0,
            tiled=True,
        ).astype(jnp.float32)
        block_rows = (middle + fed_forward + bias_down).astype(jnp.bfloat16)
        kept = (
            inputs,
            middle,
            sent_first,
            queries,
            keys_low,
            values_low,
            log_totals,
            context,
            sent_second,
            hidden_pre,
            active,
        )
        return (block_rows, kept)

    def run_ffn_back(kept, grad_row, grads, sums):
        (
            inputs,
            middle,
            sent_first,
            queries,
            keys_low,
            values_low,
            log_totals,
            context,
            sent_second,
            hidden_pre,
            active,
        ) = kept
        qkv_grad, qv_grad, out_grad, up_grad, upbias_grad, down_grad = grads
        gain_one, shift_one, outbias_grad, gain_two, shift_two, downbias_grad = sums
        grad_full = lax.all_gather(grad_row, "tensor", axis=0, tiled=True)
        down_grad = down_grad + contract_rows(active, grad_full)
        active_grad = contract_cols(grad_full, weight_down)
        gelu_pull = jax.vjp(exact_gelu, hidden_pre)[1]
        pre_grad = gelu_pull(active_grad)[0].astype(jnp.bfloat16)
        up_grad = up_grad + contract_rows(sent_second, pre_grad)
        upbias_grad = upbias_grad + jnp.sum(pre_grad.astype(jnp.float32), axis=0)
        normed_grad = lax.psum_scatter(
            contract_cols(pre_grad, weight_up).astype(jnp.bfloat16),
            "tensor",
            scatter_dimension=0,
            tiled=True,
        ).astype(jnp.float32)
        norm_pull = jax.vjp(layer_norm, middle, gain_second, shift_second)[1]
        middle_part, gain_part, shift_part = norm_pull(normed_grad)
        grad_float = grad_row.astype(jnp.float32)
        middle_grad = grad_float + middle_part
        grads = (qkv_grad, qv_grad, out_grad, up_grad, upbias_grad, down_grad)
        sums = (
            gain_one,
            shift_one,
            outbias_grad,
            gain_two + gain_part,
            shift_two + shift_part,
            downbias_grad + jnp.sum(grad_float, axis=0),
        )
        return (middle_grad, grads, sums)

    def run_attn_back(kept, middle_grad, id_row, grads, sums):
        (
            inputs,
            middle,
            sent_first,
            queries,
            keys_low,
            values_low,
            log_totals,
            context,
            sent_second,
            hidden_pre,
            active,
        ) = kept
        qkv_grad, qv_grad, out_grad, up_grad, upbias_grad, down_grad = grads
        gain_one, shift_one, outbias_grad, gain_two, shift_two, downbias_grad = sums
        middle_full = lax.all_gather(middle_grad.astype(jnp.bfloat16), "tensor", axis=0, tiled=True)
        out_grad = out_grad + contract_rows(context, middle_full)
        outbias_grad = outbias_grad + jnp.sum(middle_grad, axis=0)
        context_grad = contract_cols(middle_full, weight_out).astype(jnp.bfloat16)
        context_grad = context_grad.reshape(length, local_heads, HEAD)
        scores = attend(queries, keys_low, id_row)
        probs = jnp.exp(scores - log_totals)
        probs_low = probs.astype(jnp.bfloat16)
        probs_grad = jnp.einsum(
            "qhd,khd->hqk", context_grad, values_low, preferred_element_type=jnp.float32
        )
        values_grad = jnp.einsum(
            "hqk,qhd->khd", probs_low, context_grad, preferred_element_type=jnp.float32
        )
        values_grad = values_grad.astype(jnp.bfloat16).reshape(length, local_width)
        along = jnp.sum(probs * probs_grad, axis=-1, keepdims=True)
        scores_grad = (probs * (probs_grad - along)).astype(jnp.bfloat16)
        queries_grad = jnp.einsum(
            "hqk,khd->qhd", scores_grad, keys_low, preferred_element_type=jnp.float32
        )
        queries_grad = (queries_grad * scale).astype(jnp.bfloat16).reshape(length, local_width)
        keys_grad = jnp.einsum(
            "hqk,qhd->khd", scores_grad, queries, preferred_element_type=jnp.float32
        )
        keys_grad = (keys_grad * scale).astype(jnp.bfloat16).reshape(length, local_width)
        stacked = jnp.stack([queries_grad, keys_grad, values_grad], axis=1).reshape(
            length, 3 * local_width
        )
        qkv_grad = qkv_grad + contract_rows(sent_first, stacked)
        qv_grad = qv_grad + jnp.stack(
            [
                jnp.sum(queries_grad.astype(jnp.float32), axis=0),
                jnp.sum(values_grad.astype(jnp.float32), axis=0),
            ]
        )
        normed_grad = lax.psum_scatter(
            contract_cols(stacked, qkv_flat).astype(jnp.bfloat16),
            "tensor",
            scatter_dimension=0,
            tiled=True,
        ).astype(jnp.float32)
        norm_pull = jax.vjp(layer_norm, inputs, gain_first, shift_first)[1]
        input_part, gain_part, shift_part = norm_pull(normed_grad)
        grads = (qkv_grad, qv_grad, out_grad, up_grad, upbias_grad, down_grad)
        sums = (
            gain_one + gain_part,
            shift_one + shift_part,
            outbias_grad,
            gain_two,
            shift_two,
            downbias_grad,
        )
        return (middle_grad + input_part, grads, sums)

    def micro_step(carry, slices):
        grads, sums = carry
        x_row, id_row, grad_row = slices
        block_rows, kept = run_forward(x_row, id_row)
        middle_grad, grads, sums = run_ffn_back(kept, grad_row, grads, sums)
        input_rows, grads, sums = run_attn_back(kept, middle_grad, id_row, grads, sums)
        return ((grads, sums), (block_rows, input_rows))

    zero_grads = (
        jnp.zeros((model_width, 3 * local_width), jnp.float32),
        jnp.zeros((2, local_width), jnp.float32),
        jnp.zeros((local_width, model_width), jnp.float32),
        jnp.zeros((model_width, local_hidden), jnp.float32),
        jnp.zeros((local_hidden,), jnp.float32),
        jnp.zeros((local_hidden, model_width), jnp.float32),
    )
    zero_sums = tuple((jnp.zeros((model_width,), jnp.float32) for index_unused in range(6)))
    (grads, sums), (block_out, input_grad) = lax.scan(
        micro_step, (zero_grads, zero_sums), (tokens, segment_ids, cotangent)
    )
    qkv_grad, qv_grad, out_grad, up_grad, upbias_grad, down_grad = lax.psum(
        (grads[0], grads[1], grads[2], grads[3], grads[4], grads[5]), "dp"
    )
    totals = lax.psum((sums[0], sums[1], sums[2], sums[3], sums[4], sums[5]), ("dp", "tensor"))
    return (
        block_out,
        input_grad,
        totals[0],
        totals[1],
        qkv_grad.reshape(model_width, 3, local_width),
        qv_grad,
        out_grad,
        totals[2],
        totals[3],
        totals[4],
        up_grad,
        upbias_grad,
        down_grad,
        totals[5],
    )


def solution(mesh):
    in_specs = (
        P("dp", "tensor", None),
        P("dp", None),
        P(),
        P(),
        P(None, None, "tensor"),
        P(None, "tensor"),
        P("tensor", None),
        P(),
        P(),
        P(),
        P(None, "tensor"),
        P("tensor"),
        P("tensor", None),
        P(),
        P("dp", "tensor", None),
    )
    out_specs = (
        P("dp", "tensor", None),
        P("dp", "tensor", None),
        P(),
        P(),
        P(None, None, "tensor"),
        P(None, "tensor"),
        P("tensor", None),
        P(),
        P(),
        P(),
        P(None, "tensor"),
        P("tensor"),
        P("tensor", None),
        P(),
    )
    return jax.shard_map(body, mesh=mesh, in_specs=in_specs, out_specs=out_specs, check_vma=False)
```

profile of v0, /device:TPU:0, one launch (start us, length us, event | category | flops | bytes accessed | tf_op | source)
XLA Modules:
  0.0 844.0 jit_solution(12179509143798667119)
XLA Ops:
  9.7 701.7 %while.37 = (s32[]{:T(128)}, f32[768,576]{0,1:T(8,128)}, f32[2,192]{1,0:T(2,128)}, f32[192,768]{1,0:T(8,128)}, f32[768,768]{1,0:T(8,128)}, /*index=5*/f32[768]{0...) while((s32[]{:T(128)}, f32[768,576]{0,1:T(8,128)}, ...), condition=%wide.region_25.26_spmd.clone, body=%wide.region_0.25_spmd.clone.sunk | while | flops 13469501440 | bytes 442474240 | solution.py:248
  41.5 36.6 %all-gather.9.cloned.1.call-done = bf16[1024,768]{1,0:T(8,128)(2,1)} async-done(((bf16[256,768]{1,0:T(8,128)(2,1)}), bf16[1024,768]{1,0:T(8,128)(2,1)}) %all-gather.9.cloned.1.call-update) | async-done | bytes 1572880 | tf_op jit(solution)/shard_map/while/body/eval_jaxpr/all_gather | solution.py:67
  84.8 4.4 exponential_reduce_fusion.2
  89.4 5.0 convolution_convert_fusion.13
  97.0 34.2 %reduce-scatter.5.cloned.1.call-done = bf16[256,768]{1,0:T(8,128)(2,1)} async-done(((bf16[1024,768]{1,0:T(8,128)(2,1)}), bf16[256,768]{1,0:T(8,128)(2,1)}) %reduce-scatter.5.cloned.1.call-update) | async-done | bytes 393232 | tf_op jit(solution)/shard_map/while/body/eval_jaxpr/reduce_scatter | solution.py:84
  136.7 35.3 %all-gather.11.cloned.1.call-done = bf16[1024,768]{1,0:T(8,128)(2,1)} async-done(((bf16[256,768]{1,0:T(8,128)(2,1)}), bf16[1024,768]{1,0:T(8,128)(2,1)}) %all-gather.11.cloned.1.call-update) | async-done | bytes 1572880 | tf_op jit(solution)/shard_map/while/body/eval_jaxpr/all_gather | solution.py:92
  172.0 10.8 %multiply_convert_fusion.4 = (bf16[1024,768]{1,0:T(8,128)(2,1)}, f32[1024,768]{1,0:T(8,128)}, f32[1024,768]{1,0:T(8,128)}) fusion(f32[768]{0:T(1024)S(1)} %copy-done.35, bf16[1024,768]{1,0:T(8,128)(2,1)} %all-gather.11.cloned.1.call-done, bf16[768,768]{1,0:T(8,128)(2,1)S(1)} %copy-done.33), kind=kOutput, calls=%fused_computation.9.clone.1 | convolution fusion | flops 1259864064 | bytes 10619904 | tf_op jit(solution)/shard_map/while/body/eval_jaxpr/dot_general | solution.py:93
  182.8 26.6 %all-gather.13.cloned.1.call-done = bf16[1,1024,768]{2,1,0:T(8,128)(2,1)} async-done(((bf16[1,256,768]{2,1,0:T(8,128)(2,1)}), bf16[1,1024,768]{2,1,0:T(8,128)(2,1)}) %all-gather.13.cloned.1.call-update) | async-done | bytes 1572880 | tf_op jit(solution)/shard_map/while/body/eval_jaxpr/all_gather | solution.py:133
  209.4 6.5 convert_reduce_fusion.15
  219.8 34.2 %reduce-scatter.7.cloned.1.call-done = bf16[256,768]{1,0:T(8,128)(2,1)} async-done(((bf16[1024,768]{1,0:T(8,128)(2,1)}), bf16[256,768]{1,0:T(8,128)(2,1)}) %reduce-scatter.7.cloned.1.call-update) | async-done | bytes 393232 | tf_op jit(solution)/shard_map/while/body/eval_jaxpr/reduce_scatter | solution.py:140
  263.6 31.8 %all-gather.15.cloned.1.call-done = bf16[1024,768]{1,0:T(8,128)(2,1)} async-done(((bf16[256,768]{1,0:T(8,128)(2,1)}), bf16[1024,768]{1,0:T(8,128)(2,1)}) %all-gather.15.cloned.1.call-update) | async-done | bytes 1572880 | tf_op jit(solution)/shard_map/while/body/eval_jaxpr/all_gather | solution.py:177
  297.6 11.4 %multiply_reduce_fusion.5 = (f32[3,1024]{1,0:T(4,128)S(1)}, f32[3,1024,1024]{1,2,0:T(8,128)}) fusion(f32[3,1024,1024]{1,2,0:T(8,128)} %copy-done, f32[3,1024]{1,0:T(4,128)S(1)} %log_add_fusion.2, pred[1024,1024]{0,1:T(8,128)(4,1)S(1)} %copy-done.2, bf16[1024,3,64]{0,2,1:T(8,128)(2,1)S(1)} %bitcast.258, f32[1024,3,64]{0,2,1:T(8,128)} %bitcast.247, ...), kind=kOutput, calls=%fused_computation.1.clone.1 | convolution fusion | flops 418771968 | bytes 27419392 | tf_op jit(solution)/shard_map/while/body/eval_jaxpr/qhd,khd->hqk/dot_general | solution.py:185
  310.8 7.0 multiply_convert_fusion.5
  330.2 4.9 select_add_fusion.19
  346.2 22.3 %reduce-scatter.9.cloned.1.call-done = bf16[256,768]{1,0:T(8,128)(2,1)} async-done(((bf16[1024,768]{1,0:T(8,128)(2,1)}), bf16[256,768]{1,0:T(8,128)(2,1)}) %reduce-scatter.9.cloned.1.call-update) | async-done | bytes 393232 | tf_op jit(solution)/shard_map/while/body/eval_jaxpr/reduce_scatter | solution.py:212
  381.6 32.9 %all-gather.9.cloned.1.call-done = bf16[1024,768]{1,0:T(8,128)(2,1)} async-done(((bf16[256,768]{1,0:T(8,128)(2,1)}), bf16[1024,768]{1,0:T(8,128)(2,1)}) %all-gather.9.cloned.1.call-update) | async-done | bytes 1572880 | tf_op jit(solution)/shard_map/while/body/eval_jaxpr/all_gather | solution.py:67
  425.8 5.0 convolution_convert_fusion.13
  433.4 34.3 %reduce-scatter.5.cloned.1.call-done = bf16[256,768]{1,0:T(8,128)(2,1)} async-done(((bf16[1024,768]{1,0:T(8,128)(2,1)}), bf16[256,768]{1,0:T(8,128)(2,1)}) %reduce-scatter.5.cloned.1.call-update) | async-done | bytes 393232 | tf_op jit(solution)/shard_map/while/body/eval_jaxpr/reduce_scatter | solution.py:84
  473.1 35.2 %all-gather.11.cloned.1.call-done = bf16[1024,768]{1,0:T(8,128)(2,1)} async-done(((bf16[256,768]{1,0:T(8,128)(2,1)}), bf16[1024,768]{1,0:T(8,128)(2,1)}) %all-gather.11.cloned.1.call-update) | async-done | bytes 1572880 | tf_op jit(solution)/shard_map/while/body/eval_jaxpr/all_gather | solution.py:92
  508.4 10.8 %multiply_convert_fusion.4 = (bf16[1024,768]{1,0:T(8,128)(2,1)}, f32[1024,768]{1,0:T(8,128)}, f32[1024,768]{1,0:T(8,128)}) fusion(f32[768]{0:T(1024)S(1)} %copy-done.35, bf16[1024,768]{1,0:T(8,128)(2,1)} %all-gather.11.cloned.1.call-done, bf16[768,768]{1,0:T(8,128)(2,1)S(1)} %copy-done.33), kind=kOutput, calls=%fused_computation.9.clone.1 | convolution fusion | flops 1259864064 | bytes 10619904 | tf_op jit(solution)/shard_map/while/body/eval_jaxpr/dot_general | solution.py:93
  519.2 26.6 %all-gather.13.cloned.1.call-done = bf16[1,1024,768]{2,1,0:T(8,128)(2,1)} async-done(((bf16[1,256,768]{2,1,0:T(8,128)(2,1)}), bf16[1,1024,768]{2,1,0:T(8,128)(2,1)}) %all-gather.13.cloned.1.call-update) | async-done | bytes 1572880 | tf_op jit(solution)/shard_map/while/body/eval_jaxpr/all_gather | solution.py:133
  545.8 6.5 convert_reduce_fusion.15
  556.2 34.2 %reduce-scatter.7.cloned.1.call-done = bf16[256,768]{1,0:T(8,128)(2,1)} async-done(((bf16[1024,768]{1,0:T(8,128)(2,1)}), bf16[256,768]{1,0:T(8,128)(2,1)}) %reduce-scatter.7.cloned.1.call-update) | async-done | bytes 393232 | tf_op jit(solution)/shard_map/while/body/eval_jaxpr/reduce_scatter | solution.py:140
  600.0 31.8 %all-gather.15.cloned.1.call-done = bf16[1024,768]{1,0:T(8,128)(2,1)} async-done(((bf16[256,768]{1,0:T(8,128)(2,1)}), bf16[1024,768]{1,0:T(8,128)(2,1)}) %all-gather.15.cloned.1.call-update) | async-done | bytes 1572880 | tf_op jit(solution)/shard_map/while/body/eval_jaxpr/all_gather | solution.py:177
  634.0 11.4 %multiply_reduce_fusion.5 = (f32[3,1024]{1,0:T(4,128)S(1)}, f32[3,1024,1024]{1,2,0:T(8,128)}) fusion(f32[3,1024,1024]{1,2,0:T(8,128)} %copy-done, f32[3,1024]{1,0:T(4,128)S(1)} %log_add_fusion.2, pred[1024,1024]{0,1:T(8,128)(4,1)S(1)} %copy-done.2, bf16[1024,3,64]{0,2,1:T(8,128)(2,1)S(1)} %bitcast.258, f32[1024,3,64]{0,2,1:T(8,128)} %bitcast.247, ...), kind=kOutput, calls=%fused_computation.1.clone.1 | convolution fusion | flops 418771968 | bytes 27419392 | tf_op jit(solution)/shard_map/while/body/eval_jaxpr/qhd,khd->hqk/dot_general | solution.py:185
  647.2 7.0 multiply_convert_fusion.5
  666.6 5.7 select_add_fusion.19
  672.3 4.6 select_add_fusion.21
  685.6 18.9 %reduce-scatter.9.cloned.1.call-done = bf16[256,768]{1,0:T(8,128)(2,1)} async-done(((bf16[1024,768]{1,0:T(8,128)(2,1)}), bf16[256,768]{1,0:T(8,128)(2,1)}) %reduce-scatter.9.cloned.1.call-update) | async-done | bytes 393232 | tf_op jit(solution)/shard_map/while/body/eval_jaxpr/reduce_scatter | solution.py:212
  712.1 14.5 %all-reduce.1 = (f32[2,192]{1,0:T(2,128)}, f32[768]{0:T(1024)}) all-reduce(f32[2,192]{1,0:T(2,128)S(1)} %copy-done.30, f32[768]{0:T(1024)S(1)} %get-tuple-element.190), channel_id=1, replica_groups=mesh['dp'=8,'tensor'=4] {'dp'}, use_global_device_ids=true, to_apply=%region_29.30 | all-reduce | flops 1152 | bytes 9216 | tf_op jit(solution)/shard_map/psum | solution.py:251
  726.6 40.1 %all-reduce = (f32[768]{0:T(1024)}, f32[768]{0:T(1024)}, f32[768]{0:T(1024)}, f32[768]{0:T(1024)}, f32[768]{0:T(1024)}, /*index=5*/f32[768]{0:T(1024)}) all-reduce(f32[768]{0:T(1024)S(1)} %get-tuple-element.181, f32[768]{0:T(1024)S(1)} %get-tuple-element.182, ...), channel_id=1, replica_groups=mesh['dp'=8,'tensor'=4] {'dp','tensor'}, use_global_device_ids=true, to_apply=%region_26.27 | all-reduce | flops 4608 | bytes 36864 | tf_op jit(solution)/shard_map/psum | solution.py:254
  766.7 63.4 %all-reduce.5.cloned.1.call-done = (f32[768,3,192]{0,2,1:T(8,128)}, f32[192,768]{1,0:T(8,128)}, f32[768,768]{1,0:T(8,128)}, f32[768,768]{1,0:T(8,128)}) async-done(((f32[768,3,192]{0,2,1:T(8,128)}, f32[192,768]{1,0:T(8,128)}, f32[768,768]{1,0:T(8,128)}, f32[768,768]{1,0:T(8,128)}), (f32[768,3,192]{0,2,1:T(8,128)}, f32[192,768]{1,0:T(8,128)}, f32[768,768]{1,0:T(8,128)}, ...) | async-done | bytes 7077904 | tf_op jit(solution)/shard_map/psum | solution.py:251
  (321 shorter events, 148.1 us)
Async XLA Ops:
  33.4 47.3 %copy-start.22 = (bf16[768,576]{1,0:T(8,128)(2,1)}, bf16[768,576]{1,0:T(8,128)(2,1)S(1)}, u32[]{:S(2)}) copy-start(bf16[768,576]{1,0:T(8,128)(2,1)S(1)} %get-tuple-element.747) | copy-start | bytes 2654212 | tf_op jit(solution)/shard_map/while
  33.4 44.8 %all-gather.9.cloned.1.call-start = ((), (), s32[]{:S(2)}) async-start(), calls=%async_computation.5 | async-start | bytes 1966080 | tf_op jit(solution)/shard_map/while/body/eval_jaxpr/all_gather | solution.py:67
  38.2 93.1 %reduce-scatter.5.cloned.1.call-start = ((), (), s32[]{:S(2)}) async-start(), calls=%async_computation.6 | async-start | bytes 1966080 | tf_op jit(solution)/shard_map/while/body/eval_jaxpr/reduce_scatter | solution.py:84
  94.4 39.4 %copy-start.21 = (f32[768]{0:T(1024)S(1)}, f32[768]{0:T(1024)}, u32[]{:S(2)}) copy-start(f32[768]{0:T(1024)} %get-tuple-element.753) | copy-start | bytes 9220 | tf_op jit(solution)/shard_map/while
  94.4 39.4 %copy-start.25 = (f32[768]{0:T(1024)S(1)}, f32[768]{0:T(1024)}, u32[]{:S(2)}) copy-start(f32[768]{0:T(1024)} %get-tuple-element.754) | copy-start | bytes 9220 | tf_op jit(solution)/shard_map/while
  95.1 40.7 %copy-start.17 = (bf16[2,256,768]{2,1,0:T(8,128)(2,1)S(1)}, bf16[2,256,768]{2,1,0:T(8,128)(2,1)}, u32[]{:S(2)}) copy-start(bf16[2,256,768]{2,1,0:T(8,128)(2,1)} %get-tuple-element.750) | copy-start | bytes 2359300 | tf_op jit(solution)/shard_map/while
  96.9 75.1 %copy-start.33 = (bf16[768,768]{1,0:T(8,128)(2,1)S(1)}, bf16[768,768]{1,0:T(8,128)(2,1)}, u32[]{:S(2)}) copy-start(bf16[768,768]{1,0:T(8,128)(2,1)} %get-tuple-element.755) | copy-start | bytes 3538948 | tf_op jit(solution)/shard_map/while
  96.9 75.1 %copy-start.35 = (f32[768]{0:T(1024)S(1)}, f32[768]{0:T(1024)}, u32[]{:S(2)}) copy-start(f32[768]{0:T(1024)} %get-tuple-element.756) | copy-start | bytes 9220 | tf_op jit(solution)/shard_map/while
  96.9 75.0 %all-gather.11.cloned.1.call-start = ((), (), s32[]{:S(2)}) async-start(), calls=%async_computation.7 | async-start | bytes 1966080 | tf_op jit(solution)/shard_map/while/body/eval_jaxpr/all_gather | solution.py:92
  135.8 73.6 %all-gather.13.cloned.1.call-start = ((), (), s32[]{:S(2)}) async-start(), calls=%async_computation.8 | async-start | bytes 1966080 | tf_op jit(solution)/shard_map/while/body/eval_jaxpr/all_gather | solution.py:133
  136.7 117.3 %reduce-scatter.7.cloned.1.call-start = ((), (), s32[]{:S(2)}) async-start(), calls=%async_computation.9 | async-start | bytes 1966080 | tf_op jit(solution)/shard_map/while/body/eval_jaxpr/reduce_scatter | solution.py:140
  217.1 36.9 %copy-start.4 = (bf16[256,768]{1,0:T(8,128)(2,1)S(1)}, bf16[256,768]{1,0:T(8,128)(2,1)}, u32[]{:S(2)}) copy-start(bf16[256,768]{1,0:T(8,128)(2,1)} %reduce-scatter.5.cloned.1.call-done) | copy-start | bytes 1179652 | tf_op jit(solution)/shard_map/while
  219.7 37.3 %copy-start.7 = (bf16[1,256,768]{2,1,0:T(8,128)(2,1)S(1)}, bf16[1,256,768]{2,1,0:T(8,128)(2,1)}, u32[]{:S(2)}) copy-start(bf16[1,256,768]{2,1,0:T(8,128)(2,1)} %get-tuple-element.640) | copy-start | bytes 1179652 | tf_op jit(solution)/shard_map/while
  219.7 75.7 %all-gather.15.cloned.1.call-start = ((), (), s32[]{:S(2)}) async-start(), calls=%async_computation.10 | async-start | bytes 1966080 | tf_op jit(solution)/shard_map/while/body/eval_jaxpr/all_gather | solution.py:177
  259.2 78.9 %reduce-scatter.11.cloned.1.call-start = ((), (), s32[]{:S(2)}) async-start(), calls=%async_computation.12 | async-start | bytes 1966080 | tf_op jit(solution)/shard_map/while/body/eval_jaxpr/reduce_scatter | solution.py:95
  263.6 104.9 %reduce-scatter.9.cloned.1.call-start = ((), (), s32[]{:S(2)}) async-start(), calls=%async_computation.11 | async-start | bytes 1966080 | tf_op jit(solution)/shard_map/while/body/eval_jaxpr/reduce_scatter | solution.py:212
  373.6 43.5 %copy-start.22 = (bf16[768,576]{1,0:T(8,128)(2,1)}, bf16[768,576]{1,0:T(8,128)(2,1)S(1)}, u32[]{:S(2)}) copy-start(bf16[768,576]{1,0:T(8,128)(2,1)S(1)} %get-tuple-element.747) | copy-start | bytes 2654212 | tf_op jit(solution)/shard_map/while
  373.6 40.9 %all-gather.9.cloned.1.call-start = ((), (), s32[]{:S(2)}) async-start(), calls=%async_computation.5 | async-start | bytes 1966080 | tf_op jit(solution)/shard_map/while/body/eval_jaxpr/all_gather | solution.py:67
  378.3 89.4 %reduce-scatter.5.cloned.1.call-start = ((), (), s32[]{:S(2)}) async-start(), calls=%async_computation.6 | async-start | bytes 1966080 | tf_op jit(solution)/shard_map/while/body/eval_jaxpr/reduce_scatter | solution.py:84
  430.7 39.4 %copy-start.21 = (f32[768]{0:T(1024)S(1)}, f32[768]{0:T(1024)}, u32[]{:S(2)}) copy-start(f32[768]{0:T(1024)} %get-tuple-element.753) | copy-start | bytes 9220 | tf_op jit(solution)/shard_map/while
  430.8 39.4 %copy-start.25 = (f32[768]{0:T(1024)S(1)}, f32[768]{0:T(1024)}, u32[]{:S(2)}) copy-start(f32[768]{0:T(1024)} %get-tuple-element.754) | copy-start | bytes 9220 | tf_op jit(solution)/shard_map/while
  431.5 40.8 %copy-start.17 = (bf16[2,256,768]{2,1,0:T(8,128)(2,1)S(1)}, bf16[2,256,768]{2,1,0:T(8,128)(2,1)}, u32[]{:S(2)}) copy-start(bf16[2,256,768]{2,1,0:T(8,128)(2,1)} %get-tuple-element.750) | copy-start | bytes 2359300 | tf_op jit(solution)/shard_map/while
  433.3 75.1 %copy-start.33 = (bf16[768,768]{1,0:T(8,128)(2,1)S(1)}, bf16[768,768]{1,0:T(8,128)(2,1)}, u32[]{:S(2)}) copy-start(bf16[768,768]{1,0:T(8,128)(2,1)} %get-tuple-element.755) | copy-start | bytes 3538948 | tf_op jit(solution)/shard_map/while
  433.3 75.1 %copy-start.35 = (f32[768]{0:T(1024)S(1)}, f32[768]{0:T(1024)}, u32[]{:S(2)}) copy-start(f32[768]{0:T(1024)} %get-tuple-element.756) | copy-start | bytes 9220 | tf_op jit(solution)/shard_map/while
  433.3 75.1 %all-gather.11.cloned.1.call-start = ((), (), s32[]{:S(2)}) async-start(), calls=%async_computation.7 | async-start | bytes 1966080 | tf_op jit(solution)/shard_map/while/body/eval_jaxpr/all_gather | solution.py:92
  472.2 73.6 %all-gather.13.cloned.1.call-start = ((), (), s32[]{:S(2)}) async-start(), calls=%async_computation.8 | async-start | bytes 1966080 | tf_op jit(solution)/shard_map/while/body/eval_jaxpr/all_gather | solution.py:133
  473.1 117.3 %reduce-scatter.7.cloned.1.call-start = ((), (), s32[]{:S(2)}) async-start(), calls=%async_computation.9 | async-start | bytes 1966080 | tf_op jit(solution)/shard_map/while/body/eval_jaxpr/reduce_scatter | solution.py:140
  556.1 37.3 %copy-start.7 = (bf16[1,256,768]{2,1,0:T(8,128)(2,1)S(1)}, bf16[1,256,768]{2,1,0:T(8,128)(2,1)}, u32[]{:S(2)}) copy-start(bf16[1,256,768]{2,1,0:T(8,128)(2,1)} %get-tuple-element.640) | copy-start | bytes 1179652 | tf_op jit(solution)/shard_map/while
  556.1 75.7 %all-gather.15.cloned.1.call-start = ((), (), s32[]{:S(2)}) async-start(), calls=%async_computation.10 | async-start | bytes 1966080 | tf_op jit(solution)/shard_map/while/body/eval_jaxpr/all_gather | solution.py:177
  595.6 81.4 %reduce-scatter.11.cloned.1.call-start = ((), (), s32[]{:S(2)}) async-start(), calls=%async_computation.12 | async-start | bytes 1966080 | tf_op jit(solution)/shard_map/while/body/eval_jaxpr/reduce_scatter | solution.py:95
  600.0 104.6 %reduce-scatter.9.cloned.1.call-start = ((), (), s32[]{:S(2)}) async-start(), calls=%async_computation.11 | async-start | bytes 1966080 | tf_op jit(solution)/shard_map/while/body/eval_jaxpr/reduce_scatter | solution.py:212
  711.4 118.7 %all-reduce.5.cloned.1.call-start = ((), (), s32[]{:S(2)}) async-start(), calls=%async_computation.4 | async-start | bytes 14155776 | tf_op jit(solution)/shard_map/psum | solution.py:251
  (63 other events, 572.1 us)
Sparse Core Ops, SparseCore 0:
  38.3 39.7 all-gather.8
  97.1 34.1 reduce-scatter.4
  135.9 36.0 all-gather.10
  173.4 35.9 all-gather.12
  219.8 34.1 reduce-scatter.6
  259.3 36.0 all-gather.14
  297.7 34.1 reduce-scatter.10
  334.2 34.2 reduce-scatter.8
  378.4 36.0 all-gather.8
  433.4 34.1 reduce-scatter.4
  472.3 36.0 all-gather.10
  509.8 35.9 all-gather.12
  556.2 34.1 reduce-scatter.6
  595.7 36.0 all-gather.14
  634.0 34.1 reduce-scatter.10
  670.3 34.2 reduce-scatter.8
Sparse Core Ops, SparseCore 1:
  716.7 113.3 all-reduce.4
where the time goes:
time: 847 us; the launch traced here: 844 us
  waiting for transfers between devices  499 us (59%)
  matrix products  152 us (18%)
  other arithmetic  70.7 us (8%)
  blocking collectives  54.5 us (6%)
  loops' own time  26.6 us (3%)
  local copies, waits for them, and re-layouts  24.7 us (3%)
  between operations  15.5 us (2%)
    all_gather x2, waiting for transfers between devices, run_forward(): sent_second = lax.all_gather(normed_second, 'tensor', axis=0, tiled=True)  70.5 us
    all_gather x2, waiting for transfers between devices, run_forward(): sent_first = lax.all_gather(normed, 'tensor', axis=0, tiled=True)  69.5 us
    reduce_scatter x2, waiting for transfers between devices, run_forward(): lax.psum_scatter(jnp.dot(context, weight_out, preferred_element_type=jnp....  68.5 us
    reduce_scatter x2, waiting for transfers between devices, run_ffn_back(): lax.psum_scatter(contract_cols(pre_grad, weight_up).astype(jnp.bfloat16),...  68.5 us
    all_gather x2, waiting for transfers between devices, run_attn_back(): lax.all_gather(middle_grad.astype(jnp.bfloat16), 'tensor', axis=0, tiled=...  63.6 us
    psum x1, waiting for transfers between devices, body(): lax.psum((grads[0], grads[1], grads[2], grads[3], grads[4], grads[5]), 'dp')  63.4 us
    all_gather x2, waiting for transfers between devices, run_ffn_back(): grad_full = lax.all_gather(grad_row, 'tensor', axis=0, tiled=True)  53.2 us
    reduce_scatter x2, waiting for transfers between devices, run_attn_back(): lax.psum_scatter(contract_cols(stacked, qkv_flat).astype(jnp.bfloat16), '...  41.2 us
  transfers between devices with their start and end apart: 17, of which 15 were waited for; matrix products, arithmetic and copies ran while one was open for 16% of the time, Pallas kernels for 0%

commit v1 on v0

v1 whole, which is shorter than its diff:
```python
import functools

import jax
import jax.numpy as jnp
from jax import lax
from jax.experimental import pallas as pl
from jax.experimental.pallas import tpu as pltpu
from jax.sharding import PartitionSpec as P

HEAD = 64
PLANE = 8
LOG2E = 1.4426950408889634
BF = jnp.bfloat16
F32 = jnp.float32


def dot(left, right, dims):
    return lax.dot_general(left, right, ((dims[0], dims[1]), ((), ())), preferred_element_type=F32)


def attend_fwd_kernel(qt_ref, kt_ref, vt_ref, idq_ref, idk_ref, ct_ref, lse_ref):
    keys = kt_ref[...].T
    values_t = vt_ref[...]
    factor = HEAD**-0.5 * LOG2E
    tile = 256
    for start in range(0, qt_ref.shape[1], tile):
        cols = slice(start, start + tile)
        scores = dot(keys, qt_ref[:, cols], ((1,), (0,)))
        scores = jnp.where(idk_ref[...] == idq_ref[:, cols], scores, -1e30)
        top = jnp.max(scores, axis=0, keepdims=True)
        probs = jnp.exp2((scores - top) * factor)
        total = jnp.sum(probs, axis=0, keepdims=True)
        context = dot(values_t, probs.astype(BF), ((1,), (0,)))
        ct_ref[:, cols] = (context / total).astype(BF)
        lse_ref[0, :, cols] = top * factor + jnp.log2(total)


def attend_fwd(qt, kt, vt, idq, idk):
    width, queries = qt.shape
    keys = kt.shape[1]
    heads = width // HEAD
    return pl.pallas_call(
        attend_fwd_kernel,
        grid=(heads,),
        in_specs=[
            pl.BlockSpec((HEAD, queries), lambda h: (h, 0)),
            pl.BlockSpec((HEAD, keys), lambda h: (h, 0)),
            pl.BlockSpec((HEAD, keys), lambda h: (h, 0)),
            pl.BlockSpec((1, queries), lambda h: (0, 0)),
            pl.BlockSpec((keys, 1), lambda h: (0, 0)),
        ],
        out_specs=[
            pl.BlockSpec((HEAD, queries), lambda h: (h, 0)),
            pl.BlockSpec((1, 1, queries), lambda h: (h, 0, 0)),
        ],
        out_shape=[
            jax.ShapeDtypeStruct((width, queries), BF),
            jax.ShapeDtypeStruct((heads, 1, queries), F32),
        ],
        compiler_params=pltpu.CompilerParams(vmem_limit_bytes=40 * 2**20),
        cost_estimate=pl.CostEstimate(
            flops=16 * width * queries * keys,
            bytes_accessed=8 * width * keys,
            transcendentals=heads * queries * keys,
        ),
        name="attend_fwd",
    )(qt, kt, vt, idq, idk)


def attend_bwd_kernel(
    qt_ref, kt_ref, vt_ref, ct_ref, dct_ref, lse_ref, idq_ref, idk_ref, dqt_ref, dkt_ref, dvt_ref
):
    keys_t = kt_ref[...]
    keys = keys_t.T
    values = vt_ref[...].T
    scale = HEAD**-0.5
    tile = 256
    dkt = jnp.zeros(keys_t.shape, F32)
    dvt = jnp.zeros(keys_t.shape, F32)
    for start in range(0, qt_ref.shape[1], tile):
        cols = slice(start, start + tile)
        queries_t = qt_ref[:, cols]
        grad_t = dct_ref[:, cols]
        scores = dot(keys, queries_t, ((1,), (0,)))
        scores = jnp.where(idk_ref[...] == idq_ref[:, cols], scores, -1e30)
        probs = jnp.exp2(scores * (scale * LOG2E) - lse_ref[0, :, cols])
        along = jnp.sum(
            grad_t.astype(F32) * ct_ref[:, cols].astype(F32), axis=0, keepdims=True
        )
        probs_grad = dot(values, grad_t, ((1,), (0,)))
        scores_grad = (probs * (probs_grad - along)).astype(BF)
        dvt += dot(grad_t, probs.astype(BF), ((1,), (1,)))
        dkt += dot(queries_t, scores_grad, ((1,), (1,)))
        dqt_ref[:, cols] = (dot(keys_t, scores_grad, ((1,), (0,))) * scale).astype(BF)
    dkt_ref[...] = (dkt * scale).astype(BF)
    dvt_ref[...] = dvt.astype(BF)


def attend_bwd(qt, kt, vt, ct, dct, lse, idq, idk):
    width, queries = qt.shape
    keys = kt.shape[1]
    heads = width // HEAD
    by_queries = pl.BlockSpec((HEAD, queries), lambda h: (h, 0))
    by_keys = pl.BlockSpec((HEAD, keys), lambda h: (h, 0))
    return pl.pallas_call(
        attend_bwd_kernel,
        grid=(heads,),
        in_specs=[
            by_queries,
            by_keys,
            by_keys,
            by_queries,
            by_queries,
            pl.BlockSpec((1, 1, queries), lambda h: (h, 0, 0)),
            pl.BlockSpec((1, queries), lambda h: (0, 0)),
            pl.BlockSpec((keys, 1), lambda h: (0, 0)),
        ],
        out_specs=[by_queries, by_keys, by_keys],
        out_shape=[
            jax.ShapeDtypeStruct((width, queries), BF),
            jax.ShapeDtypeStruct((width, keys), BF),
            jax.ShapeDtypeStruct((width, keys), BF),
        ],
        compiler_params=pltpu.CompilerParams(vmem_limit_bytes=40 * 2**20),
        cost_estimate=pl.CostEstimate(
            flops=40 * width * queries * keys,
            bytes_accessed=16 * width * keys,
            transcendentals=heads * queries * keys,
        ),
        name="attend_bwd",
    )(qt, kt, vt, ct, dct, lse, idq, idk)


def layer_norm(inputs, scaling, offset):
    center = inputs - jnp.mean(inputs, axis=-1, keepdims=True)
    spread = jnp.mean(center * center, axis=-1, keepdims=True)
    return center * lax.rsqrt(spread + 1e-05) * scaling + offset


def exact_gelu(values):
    return jax.nn.gelu(values, approximate=False)


def product(form, left, right):
    return jnp.einsum(form, left, right, preferred_element_type=F32)


class Moves:
    def __init__(self, dp, lines):
        self.dp, self.lines = dp, lines
        self.t = lax.axis_index("tensor")
        self.d = lax.axis_index("dp")
        self.e = self.d % PLANE
        self.c = self.d % 2
        self.first = [(i, i ^ (2 if i % 2 == 0 else 4)) for i in range(dp)]
        self.second = [(i, i ^ (4 if i % 2 == 0 else 2)) for i in range(dp)]
        self.core = [(i, i ^ 1) for i in range(dp)]
        self.to_owner = ([], [])
        for i in range(dp):
            for z in range(lines):
                for which in range(2):
                    row = (z + which) % 2
                    target = (i - i % 2 + z // 2) * lines + 2 * (i % 2) + row
                    self.to_owner[which].append((i * lines + z, target))
        self.to_home = tuple([(b, a) for a, b in pairs] for pairs in self.to_owner)

    def flip(self, value, pairs):
        return lax.ppermute(value, "dp", pairs)

    def from_line(self, value, step):
        pairs = [((i + step) % self.lines, i) for i in range(self.lines)]
        return lax.ppermute(value, "tensor", pairs)

    def to_line(self, value, step):
        pairs = [(i, (i + step) % self.lines) for i in range(self.lines)]
        return lax.ppermute(value, "tensor", pairs)

    def rows_to_owner(self, blocks):
        even = self.t % 2 == 0
        sent = (
            jnp.where(even, blocks[0], blocks[1]),
            jnp.where(even, blocks[1], blocks[0]),
        )
        got = [lax.ppermute(sent[k], ("dp", "tensor"), self.to_owner[k]) for k in range(2)]
        return jnp.concatenate(got, axis=0)

    def rows_to_home(self, half):
        size = half.shape[0] // 2
        got = [
            lax.ppermute(half[k * size : (k + 1) * size], ("dp", "tensor"), self.to_home[k])
            for k in range(2)
        ]
        even = self.t % 2 == 0
        return jnp.stack([jnp.where(even, got[0], got[1]), jnp.where(even, got[1], got[0])])

    def plane_gather(self, piece):
        parts = [piece]
        parts += [self.flip(part, self.first) for part in parts]
        parts += [self.flip(part, self.second) for part in parts]
        parts += [self.flip(part, self.core) for part in parts]
        table = jnp.array([[0, 4, 1, 6, 2, 5, 3, 7], [0, 4, 2, 5, 1, 6, 3, 7]], jnp.int32)
        stacked = jnp.stack(parts)
        return jnp.stack(
            [
                lax.dynamic_index_in_dim(
                    stacked, table[self.c, self.e ^ place], axis=0, keepdims=False
                )
                for place in range(PLANE)
            ]
        )

    def shard_gather(self, shard):
        rows = shard.shape[0] // PLANE
        piece = lax.dynamic_slice_in_dim(shard, self.e * rows, rows, axis=0)
        pieces = jnp.stack([self.from_line(piece, s) for s in range(1, self.lines)])
        whole = self.plane_gather(pieces)
        whole = jnp.moveaxis(whole, 0, 1).reshape((self.lines - 1,) + shard.shape)
        return jnp.concatenate([shard[None], whole], axis=0)

    def shard_reduce(self, grads):
        lines, rows, width = grads.shape
        size = rows // PLANE
        parts = grads.reshape(lines, 4, 2, size, width)
        x_bit, y_bit = (self.e // 2) % 2, self.e // 4
        zero = self.c == 0

        def pick(values, index, axis):
            return lax.dynamic_index_in_dim(values, index, axis=axis, keepdims=False)

        def join(kept, got):
            return (kept.astype(F32) + got.astype(F32)).astype(BF)

        got = self.flip(pick(parts, 1 - self.c, 2), self.core)
        parts = join(pick(parts, self.c, 2), got)
        keep = [jnp.where(zero, 2 * k + x_bit, 2 * y_bit + k) for k in range(2)]
        send = [jnp.where(zero, 2 * k + 1 - x_bit, 2 * (1 - y_bit) + k) for k in range(2)]
        got = self.flip(jnp.stack([pick(parts, i, 1) for i in send], axis=1), self.first)
        parts = join(jnp.stack([pick(parts, i, 1) for i in keep], axis=1), got)
        mine = jnp.where(zero, y_bit, x_bit)
        got = self.flip(pick(parts, 1 - mine, 1), self.second)
        parts = join(pick(parts, mine, 1), got)
        total = parts[0].astype(F32)
        for s in range(1, lines):
            total = total + self.to_line(parts[s], s).astype(F32)
        if self.dp > PLANE:
            groups = [[i + PLANE * g for g in range(self.dp // PLANE)] for i in range(PLANE)]
            total = lax.psum(total, "dp", axis_index_groups=groups)
        whole = self.plane_gather(total.astype(BF))
        return whole.reshape(rows, width).astype(F32)


def body(
    dp,
    lines,
    tokens,
    segment_ids,
    gain_first,
    shift_first,
    weight_qkv,
    bias_qv,
    weight_out,
    bias_out,
    gain_second,
    shift_second,
    weight_up,
    bias_up,
    weight_down,
    bias_down,
    cotangent,
):
    moves = Moves(dp, lines)
    t, c = moves.t, moves.c
    block, width = tokens.shape[1:]
    part = weight_qkv.shape[2]
    hidden = weight_up.shape[1]
    half = 2 * block

    x_half = moves.rows_to_owner(tokens)
    qkv_all = moves.shard_gather(weight_qkv.reshape(width, 3 * part))
    low = jnp.concatenate([bias_qv.reshape(-1), bias_up])
    biases = jnp.stack([low] + [moves.from_line(low, s) for s in range(1, lines)])
    bias_q = biases[:, :part].reshape(width, 1)
    bias_v = biases[:, part : 2 * part].reshape(width, 1)
    bias_hidden = biases[:, None, 2 * part :]
    other_ids = moves.flip(segment_ids, moves.core)
    id_rows = jnp.where(c == t // 2, segment_ids, other_ids)
    id_row = lax.dynamic_index_in_dim(id_rows, t % 2, axis=0, keepdims=False).reshape(lines, block)

    def half_ids(core):
        first = lax.dynamic_index_in_dim(id_row, 2 * core + t % 2, axis=0, keepdims=False)
        second = lax.dynamic_index_in_dim(id_row, 2 * core + 1 - t % 2, axis=0, keepdims=False)
        return jnp.concatenate([first, second])

    ids_own = half_ids(c)
    idq = ids_own[None, :]
    idk = jnp.concatenate([ids_own, half_ids(1 - c)])[:, None]

    out_all = moves.shard_gather(weight_out)
    up_all = moves.shard_gather(weight_up)
    down_all = moves.shard_gather(weight_down)
    grad_half = moves.rows_to_owner(cotangent)

    inputs = x_half.astype(F32)
    normed = layer_norm(inputs, gain_first, shift_first).astype(BF)
    qkv_all = qkv_all.reshape(lines, width, 3, part)
    qkv_t = product("skjp,tk->jspt", qkv_all, normed).reshape(3, width, half)
    qt = (qkv_t[0] + bias_q).astype(BF)
    kv_own = jnp.stack([qkv_t[1], qkv_t[2] + bias_v]).astype(BF)
    kv_other = moves.flip(kv_own, moves.core)
    kt, vt = jnp.concatenate([kv_own, kv_other], axis=2)
    ct, lse = attend_fwd(qt, kt, vt, idq, idk)
    out_flat = out_all.reshape(width, width)
    middle = inputs + product("jt,jd->td", ct, out_flat) + bias_out
    normed_second = layer_norm(middle, gain_second, shift_second).astype(BF)
    hidden_pre = product("td,sdf->stf", normed_second, up_all) + bias_hidden
    active, gelu_pull = jax.vjp(exact_gelu, hidden_pre)
    active = active.astype(BF)
    fed_forward = product("stf,sfd->td", active, down_all)
    block_out = moves.rows_to_home((middle + fed_forward + bias_down).astype(BF))

    down_grad = moves.shard_reduce(product("stf,td->sfd", active, grad_half).astype(BF))
    active_grad = product("td,sfd->stf", grad_half, down_all)
    pre_grad = gelu_pull(active_grad)[0].astype(BF)
    up_grad = moves.shard_reduce(product("td,stf->sdf", normed_second, pre_grad).astype(BF))
    upbias_grad = jnp.sum(pre_grad.astype(F32), axis=1)
    normed_grad = product("stf,sdf->td", pre_grad, up_all)
    norm_pull = jax.vjp(layer_norm, middle, gain_second, shift_second)[1]
    middle_part, gain_two, shift_two = norm_pull(normed_grad)
    grad_float = grad_half.astype(F32)
    middle_grad = grad_float + middle_part

    middle_low = middle_grad.astype(BF)
    out_grad = product("jt,td->jd", ct, middle_low).astype(BF)
    out_grad = moves.shard_reduce(out_grad.reshape(lines, part, width))
    dct = product("jd,td->jt", out_flat, middle_low).astype(BF)
    dqt, dkt, dvt = attend_bwd(qt, kt, vt, ct, dct, lse, idq, idk)
    partial = jnp.stack([dkt, dvt])
    got = moves.flip(partial[:, :, half:], moves.core)
    dkv = (partial[:, :, :half].astype(F32) + got.astype(F32)).astype(BF)
    stacked = jnp.concatenate([dqt[None], dkv]).reshape(3, lines, part, half)
    qkv_grad = product("tk,jspt->skjp", normed, stacked).astype(BF)
    qkv_grad = moves.shard_reduce(qkv_grad.reshape(lines, width, 3 * part))
    normed_grad = product("jspt,skjp->tk", stacked, qkv_all)
    norm_pull = jax.vjp(layer_norm, inputs, gain_first, shift_first)[1]
    input_part, gain_one, shift_one = norm_pull(normed_grad)
    input_grad = moves.rows_to_home((middle_grad + input_part).astype(BF)).astype(F32)

    bias_sums = jnp.concatenate(
        [
            jnp.sum(dqt.astype(F32), axis=1).reshape(lines, part),
            jnp.sum(dkv[1].astype(F32), axis=1).reshape(lines, part),
            upbias_grad,
        ],
        axis=1,
    )
    sums = jnp.concatenate(
        [
            jnp.roll(bias_sums, t, axis=0).reshape(-1),
            gain_one,
            shift_one,
            jnp.sum(middle_grad, axis=0),
            gain_two,
            shift_two,
            jnp.sum(grad_float, axis=0),
        ]
    )
    sums = lax.psum(sums, ("dp", "tensor"))
    own = bias_sums.shape[1]
    mine = lax.dynamic_slice_in_dim(sums, t * own, own)
    totals = sums[lines * own :].reshape(6, width)
    return (
        block_out,
        input_grad,
        totals[0],
        totals[1],
        qkv_grad.reshape(width, 3, part),
        mine[: 2 * part].reshape(2, part),
        out_grad,
        totals[2],
        totals[3],
        totals[4],
        up_grad,
        mine[2 * part :],
        down_grad,
        totals[5],
    )


def solution(mesh):
    in_specs = (
        P("dp", "tensor", None),
        P("dp", None),
        P(),
        P(),
        P(None, None, "tensor"),
        P(None, "tensor"),
        P("tensor", None),
        P(),
        P(),
        P(),
        P(None, "tensor"),
        P("tensor"),
        P("tensor", None),
        P(),
        P("dp", "tensor", None),
    )
    out_specs = (
        P("dp", "tensor", None),
        P("dp", "tensor", None),
        P(),
        P(),
        P(None, None, "tensor"),
        P(None, "tensor"),
        P("tensor", None),
        P(),
        P(),
        P(),
        P(None, "tensor"),
        P("tensor"),
        P("tensor", None),
        P(),
    )
    whole = functools.partial(body, mesh.shape["dp"], mesh.shape["tensor"])
    return jax.shard_map(whole, mesh=mesh, in_specs=in_specs, out_specs=out_specs, check_vma=False)
```

time: 847 us -> 556 us (0.66)
  waiting for transfers between devices: 499 us -> 140 us
  starting transfers between devices: 0.7 us -> 140 us
  matrix products: 152 us -> 58.2 us
  local copies, waits for them, and re-layouts: 24.7 us -> 85.8 us
  other arithmetic: 70.7 us -> 27.9 us
  Pallas kernels: 0 us -> 38 us
  loops' own time: 26.6 us -> 0 us
  blocking collectives: 54.5 us -> 38 us
    all_gather x8 -> x0, waiting for transfers between devices: 257 us -> none  [the longest x2 70.5 us: run_forward(): sent_second = lax.all_gather(normed_second, 'tensor', axis=0, tiled=True)]
    reduce_scatter x8 -> x0, waiting for transfers between devices: 178 us -> none  [the longest x2 68.5 us: run_forward(): lax.psum_scatter(jnp.dot(context, weight_out, preferred_element_type=jnp....]
    ppermute x0 -> x106, starting transfers between devices: none -> 140 us  [the longest x71 70.3 us: flip(): return lax.ppermute(value, 'dp', pairs)]
    ppermute x0 -> x106, waiting for transfers between devices: none -> 140 us  [the longest x71 105 us: flip(): return lax.ppermute(value, 'dp', pairs)]
    dot_general x36 -> x11, matrix products: 152 us -> 55.9 us  [product(): return jnp.einsum(form, left, right, preferred_element_type=F32)]
    psum x1 -> x0, waiting for transfers between devices: 63.4 us -> none  [body(): lax.psum((grads[0], grads[1], grads[2], grads[3], grads[4], grads[5]), 'dp')]
    pallas_call x0 -> x2, Pallas kernels: none -> 38 us  [the longest x1 19 us: attend_bwd(): pl.pallas_call(attend_bwd_kernel, grid=(heads,), in_specs=[by_queries, by...]
    dynamic_slice x2 -> x12, local copies, waits for them, and re-layouts: 1.41 us -> 28.5 us  [the longest x6 24.2 us: pick(): return lax.dynamic_index_in_dim(values, index, axis=axis, keepdims=False)]
  transfers between devices with their start and end apart: 17 -> 106, of which waited for: 15 -> 42; matrix products, arithmetic and copies ran while one was open for 16% -> 21% of each run, Pallas kernels for 0% -> 0%
where the time goes in v1:
time: 556 us; the launch traced here: 547 us
  starting transfers between devices  140 us (25%)
  waiting for transfers between devices  140 us (25%)
  local copies, waits for them, and re-layouts  85.8 us (15%)
  matrix products  58.2 us (10%)
  Pallas kernels  38 us (7%)
  blocking collectives  38 us (7%)
  other arithmetic  27.9 us (5%)
  between operations  19.2 us (3%)
    ppermute x71, waiting for transfers between devices, flip(): return lax.ppermute(value, 'dp', pairs)  105 us
    ppermute x71, starting transfers between devices, flip(): return lax.ppermute(value, 'dp', pairs)  70.3 us
    dot_general x11, matrix products, product(): return jnp.einsum(form, left, right, preferred_element_type=F32)  55.9 us
    psum x1, blocking collectives, body(): sums = lax.psum(sums, ('dp', 'tensor'))  38 us
    ppermute x12, starting transfers between devices, to_line(): return lax.ppermute(value, 'tensor', pairs)  32.7 us
    ppermute x15, starting transfers between devices, from_line(): return lax.ppermute(value, 'tensor', pairs)  25.5 us
    dynamic_slice x6, local copies, waits for them, and re-layouts, pick(): return lax.dynamic_index_in_dim(values, index, axis=axis, keepdims=False)  24.2 us
    unnamed x230, local copies, waits for them, and re-layouts  23.4 us
  transfers between devices with their start and end apart: 106, of which 42 were waited for; matrix products, arithmetic and copies ran while one was open for 21% of the time, Pallas kernels for 0%

profile of v1, /device:TPU:0, one launch (start us, length us, event | category | flops | bytes accessed | tf_op | source)
XLA Modules:
  0.0 546.6 jit_solution(16025628149991949342)
XLA Ops:
  42.1 7.4 %collective-permute-done.4 = bf16[96,576]{0,1:T(8,128)(2,1)S(1)} collective-permute-done((bf16[96,576]{0,1:T(8,128)(2,1)S(1)}, bf16[96,576]{0,1:T(8,128)(2,1)S(1)}, u32[]{:S(2)}, u32[]{:S(2)}) %collective-permute-start.4) | collective-permute-done | bytes 110624 | tf_op jit(solution)/shard_map/ppermute | solution.py:172
  49.5 9.1 %collective-permute-done.3 = bf16[96,576]{0,1:T(8,128)(2,1)S(1)} collective-permute-done((bf16[96,576]{0,1:T(8,128)(2,1)S(1)}, bf16[96,576]{0,1:T(8,128)(2,1)S(1)}, u32[]{:S(2)}, u32[]{:S(2)}) %collective-permute-start.3) | collective-permute-done | bytes 110624 | tf_op jit(solution)/shard_map/ppermute | solution.py:172
  58.5 4.5 collective-permute-start.29
  100.5 5.2 collective-permute-done.5
  105.6 10.5 %collective-permute-start.43 = (bf16[3,96,768]{2,1,0:T(8,128)(2,1)S(1)}, bf16[3,96,768]{2,1,0:T(8,128)(2,1)S(1)}, u32[]{:S(2)}, u32[]{:S(2)}) collective-permute-start(bf16[3,96,768]{2,1,0:T(8,128)(2,1)S(1)} %pad_maximum_fusion.23), channel_id=1, source_target_pairs={{0,4},{4,0},{8,12},{12,8},{16,20},{20,16},{24,28},{28,24},{1,5},{5... | collective-permute-start | bytes 1327112 | tf_op jit(solution)/shard_map/ppermute | solution.py:168
  117.5 9.3 %collective-permute-start.33 = (bf16[3,96,768]{2,1,0:T(8,128)(2,1)S(1)}, bf16[3,96,768]{2,1,0:T(8,128)(2,1)S(1)}, u32[]{:S(2)}, u32[]{:S(2)}) collective-permute-start(bf16[3,96,768]{2,1,0:T(8,128)(2,1)S(1)} %pad_maximum_fusion.22), channel_id=1, source_target_pairs={{0,4},{4,0},{8,12},{12,8},{16,20},{20,16},{24,28},{28,24},{1,5},{5... | collective-permute-start | bytes 1327112 | tf_op jit(solution)/shard_map/ppermute | solution.py:168
  132.8 5.4 collective-permute-done.7
  142.9 6.4 %collective-permute-done.42 = bf16[3,96,768]{2,1,0:T(8,128)(2,1)} collective-permute-done((bf16[3,96,768]{2,1,0:T(8,128)(2,1)S(1)}, bf16[3,96,768]{2,1,0:T(8,128)(2,1)}, u32[]{:S(2)}, u32[]{:S(2)}) %collective-permute-start.42) | collective-permute-done | bytes 442400 | tf_op jit(solution)/shard_map/ppermute | solution.py:168
  153.0 6.5 %collective-permute-done.32 = bf16[3,96,768]{2,1,0:T(8,128)(2,1)} collective-permute-done((bf16[3,96,768]{2,1,0:T(8,128)(2,1)S(1)}, bf16[3,96,768]{2,1,0:T(8,128)(2,1)}, u32[]{:S(2)}, u32[]{:S(2)}) %collective-permute-start.32) | collective-permute-done | bytes 442400 | tf_op jit(solution)/shard_map/ppermute | solution.py:168
  163.3 4.1 copy.130
  167.3 5.5 %concatenate.56 = bf16[3,768,3,192]{1,3,2,0:T(8,128)(2,1)S(1)} reshape(bf16[3,8,96,576]{2,1,3,0:T(8,128)(2,1)} %copy.130) | data formatting | bytes 5308416 | tf_op jit(solution)/shard_map/concatenate | solution.py:218
  184.5 19.0 %attend_fwd.1 = (bf16[768,512]{1,0:T(8,128)(2,1)S(1)}, f32[12,1,512]{2,1,0:T(1,128)S(1)}) custom-call(bf16[768,512]{1,0:T(8,128)(2,1)S(1)} %fusion.46.qt_ref, bf16[768,1024]{1,0:T(8,128)(2,1)S(1)} %get-tuple-element.50.kt_ref, bf16[768,1024]{1,0:T(8,128)(2,1)S(1)} %get-tuple-element.49.vt_ref, s32[1,512]{1,0:T(1,128)S(1)} %bitcast.476, ...), custom_call_target="tpu_custom_call" | custom-call | flops 6442450944 | bytes 6291456 | tf_op jit(solution)/shard_map/attend_fwd/pallas_call | solution.py:42
  204.9 18.9 %fusion.9 = (bf16[4,512,768]{2,1,0:T(8,128)(2,1)S(1)}, f32[4,512,768]{2,1,0:T(8,128)}, f32[4,768,512]{1,2,0:T(8,128)}) fusion(f32[4,768]{1,0:T(4,128)S(1)} %pad_maximum_fusion.26, bf16[3,768,768]{2,1,0:T(8,128)(2,1)S(1)} %bitcast.490, bf16[1,768,768]{2,1,0:T(8,128)(2,1)S(1)} %bitcast.531, f32[512,768]{1,0:T(8,128)S(1)} %get-tuple-element.114, ...), kind=kOutput, calls=%fused_computation.17 | convolution fusion | flops 2531131392 | bytes 22042624 | tf_op jit(solution)/shard_map/td,sdf->stf/dot_general | solution.py:145
  223.9 10.9 %convert_reduce_fusion = (f32[4,768]{1,0:T(4,128)}, bf16[4,512,768]{2,1,0:T(8,128)(2,1)}) fusion(f32[4,512,768]{2,1,0:T(8,128)} %get-tuple-element.44, bf16[512,768]{1,0:T(8,128)(2,1)S(1)} %copy-done.25, bf16[3,768,768]{2,1,0:T(8,128)(2,1)S(1)} %bitcast.488, bf16[1,768,768]{2,1,0:T(8,128)(2,1)S(1)} %bitcast.533, f32[4,768,512]{1,2,0:T(8,128)} %get-tuple-element.115, ...), kind=kOutput, calls=%fused_computation.18 | convolution fusion | flops 2445014016 | bytes 21258240 | tf_op jit(solution)/shard_map/td,sfd->stf/dot_general | solution.py:145
  234.8 5.4 fusion.43
  247.4 19.0 %attend_bwd.1 = (bf16[768,512]{1,0:T(8,128)(2,1)S(1)}, bf16[768,1024]{1,0:T(8,128)(2,1)S(1)}, bf16[768,1024]{1,0:T(8,128)(2,1)S(1)}) custom-call(bf16[768,512]{1,0:T(8,128)(2,1)S(1)} %fusion.46.qt_ref, bf16[768,1024]{1,0:T(8,128)(2,1)S(1)} %get-tuple-element.50.kt_ref, bf16[768,1024]{1,0:T(8,128)(2,1)S(1)} %get-tuple-element.49.vt_ref, ...), custom_call_target="tpu_custom_call" | custom-call | flops 16106127360 | bytes 12582912 | tf_op jit(solution)/shard_map/attend_bwd/pallas_call | solution.py:105
  274.4 4.8 collective-permute-start.67
  331.7 6.1 %reshape_reshape.6 = bf16[4,4,2,96,576]{3,2,1,4,0:T(2,128)(2,1)} reshape(bf16[4,768,3,192]{1,3,2,0:T(8,128)(2,1)S(1)} %copy.143) | data formatting | bytes 7077888 | tf_op jit(solution)/shard_map/reshape;reshape | solution.py:223
  337.8 12.7 %constant_dynamic-slice_fusion.14 = (bf16[4,4,1,96,576]{3,2,1,4,0:T(2,128)(2,1)}, bf16[4,4,1,96,576]{3,2,1,4,0:T(2,128)(2,1)}) fusion(bf16[4,4,2,96,576]{3,2,1,4,0:T(2,128)(2,1)} %reshape_reshape.6, s32[]{:T(128)S(6)} %select_n.594, s32[]{:T(128)S(6)} %select_n.654), kind=kLoop, calls=%fused_computation.329 | loop fusion | bytes 7077896 | tf_op jit(solution)/shard_map/jit(dynamic_index_in_dim)/dynamic_slice | solution.py:228
  350.5 10.9 %copy.145 = bf16[4,4,1,96,576]{4,3,1,0,2:T(8,128)(2,1)} copy(bf16[4,4,1,96,576]{3,2,1,4,0:T(2,128)(2,1)} %get-tuple-element.46) | data formatting | bytes 3538944 | tf_op jit(solution)/shard_map/jit(dynamic_index_in_dim)/dynamic_slice | solution.py:228
  361.9 4.1 bitcast_reduce_fusion
  369.0 38.0 %psum.7 = f32[9216]{0:T(1024)S(1)} all-reduce(f32[9216]{0:T(1024)S(1)} %constant_dynamic-update-slice_fusion.84), channel_id=1, replica_groups=mesh['dp'=8,'tensor'=4] {'dp','tensor'}, use_global_device_ids=true, to_apply=%region_17.18 | all-reduce | flops 9216 | bytes 73728 | tf_op jit(solution)/shard_map/psum | solution.py:367
  411.6 9.4 %copy.155 = bf16[4,4,1,96,576]{4,3,1,0,2:T(8,128)(2,1)S(1)} copy(bf16[4,4,1,96,576]{3,2,1,4,0:T(2,128)(2,1)} %get-tuple-element.45) | data formatting | bytes 3538944
  433.4 7.4 %collective-permute-done.81 = bf16[4,2,96,768]{3,2,1,0:T(8,128)(2,1)S(1)} collective-permute-done((bf16[4,2,96,768]{3,2,1,0:T(8,128)(2,1)S(1)}, bf16[4,2,96,768]{3,2,1,0:T(8,128)(2,1)S(1)}, u32[]{:S(2)}, u32[]{:S(2)}) %collective-permute-start.81) | collective-permute-done | bytes 1179680 | tf_op jit(solution)/shard_map/ppermute | solution.py:168
  443.5 16.2 %collective-permute-done.94 = bf16[4,2,96,768]{3,2,1,0:T(8,128)(2,1)S(1)} collective-permute-done((bf16[4,2,96,768]{3,2,1,0:T(8,128)(2,1)S(1)}, bf16[4,2,96,768]{3,2,1,0:T(8,128)(2,1)S(1)}, u32[]{:S(2)}, u32[]{:S(2)}) %collective-permute-start.94) | collective-permute-done | bytes 1179680 | tf_op jit(solution)/shard_map/ppermute | solution.py:168
  463.3 11.6 %collective-permute-start.85 = (bf16[96,768]{1,0:T(8,128)(2,1)S(1)}, bf16[96,768]{1,0:T(8,128)(2,1)S(1)}, u32[]{:S(2)}, u32[]{:S(2)}) collective-permute-start(bf16[96,768]{1,0:T(8,128)(2,1)S(1)} %get-tuple-element.80), channel_id=1, source_target_pairs={{0,3},{1,0},{2,1},{3,2},{4,7},{5,4},{6,5},{7,6},{8,11},{9,8},{10,9... | collective-permute-start | bytes 442376 | tf_op jit(solution)/shard_map/ppermute | solution.py:176
  480.7 7.7 %collective-permute-start.98 = (bf16[96,768]{1,0:T(8,128)(2,1)S(1)}, bf16[96,768]{1,0:T(8,128)(2,1)S(1)}, u32[]{:S(2)}, u32[]{:S(2)}) collective-permute-start(bf16[96,768]{1,0:T(8,128)(2,1)S(1)} %get-tuple-element.77), channel_id=1, source_target_pairs={{0,3},{1,0},{2,1},{3,2},{4,7},{5,4},{6,5},{7,6},{8,11},{9,8},{10,9... | collective-permute-start | bytes 442376 | tf_op jit(solution)/shard_map/ppermute | solution.py:176
  491.3 4.0 collective-permute-done.97
  502.7 4.8 collective-permute-done.88
  509.5 4.8 collective-permute-done.101
  524.9 5.3 collective-permute-done.58
  537.4 4.0 collective-permute-done.62
  (565 shorter events, 228.7 us)
Async XLA Ops:
  2.2 29.3 %collective-permute-start.14 = (f32[1152]{0:T(1024)S(1)}, f32[1152]{0:T(1024)S(1)}, u32[]{:S(2)}, u32[]{:S(2)}) collective-permute-start(f32[1152]{0:T(1024)S(1)} %constant_dynamic-update-slice_fusion.90), channel_id=1, source_target_pairs={{3,0},{0,1},{1,2},{2,3},{7,4},{4,5},{5,6},{6,7},{11,8},{8,9},{9,10... | collective-permute-start | bytes 13832 | tf_op jit(solution)/shard_map/ppermute | solution.py:172
  5.2 29.1 %collective-permute-start.13 = (f32[1152]{0:T(1024)S(1)}, f32[1152]{0:T(1024)S(1)}, u32[]{:S(2)}, u32[]{:S(2)}) collective-permute-start(f32[1152]{0:T(1024)S(1)} %constant_dynamic-update-slice_fusion.90), channel_id=1, source_target_pairs={{2,0},{3,1},{0,2},{1,3},{6,4},{7,5},{4,6},{5,7},{10,8},{11,9},{8,1... | collective-permute-start | bytes 13832 | tf_op jit(solution)/shard_map/ppermute | solution.py:172
  7.8 26.7 %collective-permute-start.12 = (f32[1152]{0:T(1024)S(1)}, f32[1152]{0:T(1024)S(1)}, u32[]{:S(2)}, u32[]{:S(2)}) collective-permute-start(f32[1152]{0:T(1024)S(1)} %constant_dynamic-update-slice_fusion.90), channel_id=1, source_target_pairs={{1,0},{2,1},{3,2},{0,3},{5,4},{6,5},{7,6},{4,7},{9,8},{10,9},{11,1... | collective-permute-start | bytes 13832 | tf_op jit(solution)/shard_map/ppermute | solution.py:172
  10.0 28.0 %collective-permute-start.19 = (bf16[24,768]{1,0:T(8,128)(2,1)S(1)}, bf16[24,768]{1,0:T(8,128)(2,1)S(1)}, u32[]{:S(2)}, u32[]{:S(2)}) collective-permute-start(bf16[24,768]{1,0:T(8,128)(2,1)S(1)} %constant_dynamic-slice_fusion.21), channel_id=1, source_target_pairs={{3,0},{0,1},{1,2},{2,3},{7,4},{4,5},{5,6},{6,7},{11,8},{8,9},{9,10... | collective-permute-start | bytes 110600 | tf_op jit(solution)/shard_map/ppermute | solution.py:172
  10.6 29.0 %collective-permute-start.18 = (bf16[24,768]{1,0:T(8,128)(2,1)S(1)}, bf16[24,768]{1,0:T(8,128)(2,1)S(1)}, u32[]{:S(2)}, u32[]{:S(2)}) collective-permute-start(bf16[24,768]{1,0:T(8,128)(2,1)S(1)} %constant_dynamic-slice_fusion.21), channel_id=1, source_target_pairs={{2,0},{3,1},{0,2},{1,3},{6,4},{7,5},{4,6},{5,7},{10,8},{11,9},{8,1... | collective-permute-start | bytes 110600 | tf_op jit(solution)/shard_map/ppermute | solution.py:172
  34.5 36.7 %collective-permute-start.39 = (bf16[96,768]{1,0:T(8,128)(2,1)S(1)}, bf16[96,768]{1,0:T(8,128)(2,1)S(1)}, u32[]{:S(2)}, u32[]{:S(2)}) collective-permute-start(bf16[96,768]{1,0:T(8,128)(2,1)S(1)} %constant_dynamic-slice_fusion.19), channel_id=1, source_target_pairs={{3,0},{0,1},{1,2},{2,3},{7,4},{4,5},{5,6},{6,7},{11,8},{8,9},{9,10... | collective-permute-start | bytes 442376 | tf_op jit(solution)/shard_map/ppermute | solution.py:172
  35.6 35.6 %collective-permute-start.38 = (bf16[96,768]{1,0:T(8,128)(2,1)S(1)}, bf16[96,768]{1,0:T(8,128)(2,1)S(1)}, u32[]{:S(2)}, u32[]{:S(2)}) collective-permute-start(bf16[96,768]{1,0:T(8,128)(2,1)S(1)} %constant_dynamic-slice_fusion.19), channel_id=1, source_target_pairs={{2,0},{3,1},{0,2},{1,3},{6,4},{7,5},{4,6},{5,7},{10,8},{11,9},{8,1... | collective-permute-start | bytes 442376 | tf_op jit(solution)/shard_map/ppermute | solution.py:172
  40.7 22.3 %collective-permute-start.2 = (bf16[96,576]{0,1:T(8,128)(2,1)S(1)}, bf16[96,576]{0,1:T(8,128)(2,1)S(1)}, u32[]{:S(2)}, u32[]{:S(2)}) collective-permute-start(bf16[96,576]{0,1:T(8,128)(2,1)S(1)} %constant_dynamic-slice_fusion.27), channel_id=1, source_target_pairs={{1,0},{2,1},{3,2},{0,3},{5,4},{6,5},{7,6},{4,7},{9,8},{10,9},{11,1... | collective-permute-start | bytes 331784 | tf_op jit(solution)/shard_map/ppermute | solution.py:172
  49.5 22.5 %collective-permute-start.37 = (bf16[96,768]{1,0:T(8,128)(2,1)S(1)}, bf16[96,768]{1,0:T(8,128)(2,1)S(1)}, u32[]{:S(2)}, u32[]{:S(2)}) collective-permute-start(bf16[96,768]{1,0:T(8,128)(2,1)S(1)} %constant_dynamic-slice_fusion.19), channel_id=1, source_target_pairs={{1,0},{2,1},{3,2},{0,3},{5,4},{6,5},{7,6},{4,7},{9,8},{10,9},{11,1... | collective-permute-start | bytes 442376 | tf_op jit(solution)/shard_map/ppermute | solution.py:172
  71.2 24.8 %collective-permute-start = (bf16[256,768]{1,0:T(8,128)(2,1)S(1)}, bf16[256,768]{1,0:T(8,128)(2,1)S(1)}, u32[]{:S(2)}, u32[]{:S(2)}) collective-permute-start(bf16[256,768]{1,0:T(8,128)(2,1)S(1)} %get-tuple-element.74), channel_id=1, source_target_pairs={{0,0},{1,1},{2,4},{3,5},{4,2},{5,3},{6,6},{7,7},{8,8},{9,9},{10,12... | collective-permute-start | bytes 1179656 | tf_op jit(solution)/shard_map/ppermute | solution.py:184
  71.9 25.6 %collective-permute-start.1 = (bf16[256,768]{1,0:T(8,128)(2,1)S(1)}, bf16[256,768]{1,0:T(8,128)(2,1)S(1)}, u32[]{:S(2)}, u32[]{:S(2)}) collective-permute-start(bf16[256,768]{1,0:T(8,128)(2,1)S(1)} %get-tuple-element.75), channel_id=1, source_target_pairs={{0,1},{1,0},{2,5},{3,4},{4,3},{5,2},{6,7},{7,6},{8,9},{9,8},{10,13... | collective-permute-start | bytes 1179656 | tf_op jit(solution)/shard_map/ppermute | solution.py:184
  74.1 24.8 %collective-permute-start.50 = (bf16[256,768]{1,0:T(8,128)(2,1)S(1)}, bf16[256,768]{1,0:T(8,128)(2,1)S(1)}, u32[]{:S(2)}, u32[]{:S(2)}) collective-permute-start(bf16[256,768]{1,0:T(8,128)(2,1)S(1)} %get-tuple-element.68), channel_id=1, source_target_pairs={{0,1},{1,0},{2,5},{3,4},{4,3},{5,2},{6,7},{7,6},{8,9},{9,8},{10,13... | collective-permute-start | bytes 1179656 | tf_op jit(solution)/shard_map/ppermute | solution.py:184
  77.2 20.5 %collective-permute-start.49 = (bf16[256,768]{1,0:T(8,128)(2,1)S(1)}, bf16[256,768]{1,0:T(8,128)(2,1)S(1)}, u32[]{:S(2)}, u32[]{:S(2)}) collective-permute-start(bf16[256,768]{1,0:T(8,128)(2,1)S(1)} %get-tuple-element.69), channel_id=1, source_target_pairs={{0,0},{1,1},{2,4},{3,5},{4,2},{5,3},{6,6},{7,7},{8,8},{9,9},{10,12... | collective-permute-start | bytes 1179656 | tf_op jit(solution)/shard_map/ppermute | solution.py:184
  93.2 22.9 %collective-permute-start.6 = (bf16[3,96,576]{1,2,0:T(8,128)(2,1)S(1)}, bf16[3,96,576]{1,2,0:T(8,128)(2,1)S(1)}, u32[]{:S(2)}, u32[]{:S(2)}) collective-permute-start(bf16[3,96,576]{1,2,0:T(8,128)(2,1)S(1)} %pad_maximum_fusion.21), channel_id=1, source_target_pairs={{0,16},{4,12},{8,24},{12,4},{16,0},{20,28},{24,8},{28,20},{1,17},{... | collective-permute-start | bytes 995336 | tf_op jit(solution)/shard_map/ppermute | solution.py:168
  97.6 42.0 %collective-permute-start.8 = (bf16[3,96,576]{1,2,0:T(8,128)(2,1)S(1)}, bf16[3,96,576]{1,2,0:T(8,128)(2,1)S(1)}, u32[]{:S(2)}, u32[]{:S(2)}) collective-permute-start(bf16[3,96,576]{1,2,0:T(8,128)(2,1)S(1)} %pad_maximum_fusion.21), channel_id=1, source_target_pairs={{0,4},{4,0},{8,12},{12,8},{16,20},{20,16},{24,28},{28,24},{1,5},{5... | collective-permute-start | bytes 995336 | tf_op jit(solution)/shard_map/ppermute | solution.py:168
  97.8 19.7 %collective-permute-start.41 = (bf16[3,96,768]{2,1,0:T(8,128)(2,1)S(1)}, bf16[3,96,768]{2,1,0:T(8,128)(2,1)S(1)}, u32[]{:S(2)}, u32[]{:S(2)}) collective-permute-start(bf16[3,96,768]{2,1,0:T(8,128)(2,1)S(1)} %pad_maximum_fusion.23), channel_id=1, source_target_pairs={{0,16},{4,12},{8,24},{12,4},{16,0},{20,28},{24,8},{28,20},{1,17},{... | collective-permute-start | bytes 1327112 | tf_op jit(solution)/shard_map/ppermute | solution.py:168
  105.6 44.7 %collective-permute-start.43 = (bf16[3,96,768]{2,1,0:T(8,128)(2,1)S(1)}, bf16[3,96,768]{2,1,0:T(8,128)(2,1)S(1)}, u32[]{:S(2)}, u32[]{:S(2)}) collective-permute-start(bf16[3,96,768]{2,1,0:T(8,128)(2,1)S(1)} %pad_maximum_fusion.23), channel_id=1, source_target_pairs={{0,4},{4,0},{8,12},{12,8},{16,20},{20,16},{24,28},{28,24},{1,5},{5... | collective-permute-start | bytes 1327112 | tf_op jit(solution)/shard_map/ppermute | solution.py:168
  117.5 43.1 %collective-permute-start.33 = (bf16[3,96,768]{2,1,0:T(8,128)(2,1)S(1)}, bf16[3,96,768]{2,1,0:T(8,128)(2,1)S(1)}, u32[]{:S(2)}, u32[]{:S(2)}) collective-permute-start(bf16[3,96,768]{2,1,0:T(8,128)(2,1)S(1)} %pad_maximum_fusion.22), channel_id=1, source_target_pairs={{0,4},{4,0},{8,12},{12,8},{16,20},{20,16},{24,28},{28,24},{1,5},{5... | collective-permute-start | bytes 1327112 | tf_op jit(solution)/shard_map/ppermute | solution.py:168
  160.5 20.8 %collective-permute-start.36 = (bf16[3,96,768]{2,1,0:T(8,128)(2,1)}, bf16[3,96,768]{2,1,0:T(8,128)(2,1)}, u32[]{:S(2)}, u32[]{:S(2)}) collective-permute-start(bf16[3,96,768]{2,1,0:T(8,128)(2,1)} %collective-permute-done.32), channel_id=1, source_target_pairs={{0,4},{4,0},{8,12},{12,8},{16,20},{20,16},{24,28},{28,24},{1,5},{5... | collective-permute-start | bytes 1327112 | tf_op jit(solution)/shard_map/ppermute | solution.py:168
  268.3 32.8 %collective-permute-start.47 = (bf16[256,768]{1,0:T(8,128)(2,1)}, bf16[256,768]{1,0:T(8,128)(2,1)S(1)}, u32[]{:S(2)}, u32[]{:S(2)}) collective-permute-start(bf16[256,768]{1,0:T(8,128)(2,1)} %get-tuple-element.72), channel_id=1, source_target_pairs={{0,0},{1,1},{4,2},{5,3},{2,4},{3,5},{6,6},{7,7},{8,8},{9,9},{12,10... | collective-permute-start | bytes 1179656 | tf_op jit(solution)/shard_map/ppermute | solution.py:190
  269.9 34.6 %collective-permute-start.48 = (bf16[256,768]{1,0:T(8,128)(2,1)S(1)}, bf16[256,768]{1,0:T(8,128)(2,1)S(1)}, u32[]{:S(2)}, u32[]{:S(2)}) collective-permute-start(bf16[256,768]{1,0:T(8,128)(2,1)S(1)} %get-tuple-element.73), channel_id=1, source_target_pairs={{1,0},{0,1},{5,2},{4,3},{3,4},{2,5},{7,6},{6,7},{9,8},{8,9},{13,10... | collective-permute-start | bytes 1179656 | tf_op jit(solution)/shard_map/ppermute | solution.py:190
  279.4 44.6 %collective-permute-start.51 = (bf16[2,768,512]{2,1,0:T(8,128)(2,1)S(1)}, bf16[2,768,512]{2,1,0:T(8,128)(2,1)S(1)}, u32[]{:S(2)}, u32[]{:S(2)}) collective-permute-start(bf16[2,768,512]{2,1,0:T(8,128)(2,1)S(1)} %pad_maximum_fusion.9), channel_id=1, source_target_pairs={{0,4},{4,0},{8,12},{12,8},{16,20},{20,16},{24,28},{28,24},{1,5},{5... | collective-permute-start | bytes 4718600 | tf_op jit(solution)/shard_map/ppermute | solution.py:168
  287.4 133.6 %collective-permute-start.80 = (bf16[4,4,96,768]{3,2,1,0:T(8,128)(2,1)}, bf16[4,4,96,768]{3,2,1,0:T(8,128)(2,1)}, u32[]{:S(2)}, u32[]{:S(2)}) collective-permute-start(bf16[4,4,96,768]{3,2,1,0:T(8,128)(2,1)} %dynamic-slice_bitcast_fusion.1), channel_id=1, source_target_pairs={{0,4},{4,0},{8,12},{12,8},{16,20},{20,16},{24,28},{28,24},{1,5},{5... | collective-permute-start | bytes 7077896 | tf_op jit(solution)/shard_map/ppermute | solution.py:168
  306.5 120.0 %collective-permute-start.93 = (bf16[4,4,96,768]{3,2,1,0:T(8,128)(2,1)}, bf16[4,4,96,768]{3,2,1,0:T(8,128)(2,1)}, u32[]{:S(2)}, u32[]{:S(2)}) collective-permute-start(bf16[4,4,96,768]{3,2,1,0:T(8,128)(2,1)} %dynamic-slice_bitcast_fusion), channel_id=1, source_target_pairs={{0,4},{4,0},{8,12},{12,8},{16,20},{20,16},{24,28},{28,24},{1,5},{5... | collective-permute-start | bytes 7077896 | tf_op jit(solution)/shard_map/ppermute | solution.py:168
  361.5 69.9 %collective-permute-start.54 = (bf16[4,4,96,576]{3,2,1,0:T(8,128)(2,1)}, bf16[4,4,96,576]{3,2,1,0:T(8,128)(2,1)}, u32[]{:S(2)}, u32[]{:S(2)}) collective-permute-start(bf16[4,4,96,576]{3,2,1,0:T(8,128)(2,1)} %bitcast.497), channel_id=1, source_target_pairs={{0,4},{4,0},{8,12},{12,8},{16,20},{20,16},{24,28},{28,24},{1,5},{5... | collective-permute-start | bytes 5308424 | tf_op jit(solution)/shard_map/ppermute | solution.py:168
  408.5 21.6 %collective-permute-start.52 = (bf16[256,768]{1,0:T(8,128)(2,1)S(1)}, bf16[256,768]{1,0:T(8,128)(2,1)S(1)}, u32[]{:S(2)}, u32[]{:S(2)}) collective-permute-start(bf16[256,768]{1,0:T(8,128)(2,1)S(1)} %get-tuple-element.66), channel_id=1, source_target_pairs={{0,0},{1,1},{4,2},{5,3},{2,4},{3,5},{6,6},{7,7},{8,8},{9,9},{12,10... | collective-permute-start | bytes 1179656 | tf_op jit(solution)/shard_map/ppermute | solution.py:190
  409.4 20.7 %collective-permute-start.53 = (bf16[256,768]{1,0:T(8,128)(2,1)S(1)}, bf16[256,768]{1,0:T(8,128)(2,1)S(1)}, u32[]{:S(2)}, u32[]{:S(2)}) collective-permute-start(bf16[256,768]{1,0:T(8,128)(2,1)S(1)} %get-tuple-element.67), channel_id=1, source_target_pairs={{1,0},{0,1},{5,2},{4,3},{3,4},{2,5},{7,6},{6,7},{9,8},{8,9},{13,10... | collective-permute-start | bytes 1179656 | tf_op jit(solution)/shard_map/ppermute | solution.py:190
  430.0 29.8 %collective-permute-start.94 = (bf16[4,2,96,768]{3,2,1,0:T(8,128)(2,1)S(1)}, bf16[4,2,96,768]{3,2,1,0:T(8,128)(2,1)S(1)}, u32[]{:S(2)}, u32[]{:S(2)}) collective-permute-start(bf16[4,2,96,768]{3,2,1,0:T(8,128)(2,1)S(1)} %pad_maximum_fusion.17), channel_id=1, source_target_pairs={{0,8},{4,20},{8,0},{12,28},{16,24},{20,4},{24,16},{28,12},{1,9},{5... | collective-permute-start | bytes 3538952 | tf_op jit(solution)/shard_map/ppermute | solution.py:168
  441.1 21.9 %collective-permute-start.82 = (bf16[4,96,768]{2,1,0:T(8,128)(2,1)S(1)}, bf16[4,96,768]{2,1,0:T(8,128)(2,1)S(1)}, u32[]{:S(2)}, u32[]{:S(2)}) collective-permute-start(bf16[4,96,768]{2,1,0:T(8,128)(2,1)S(1)} %dynamic-slice_bitcast_fusion.3), channel_id=1, source_target_pairs={{0,16},{4,12},{8,24},{12,4},{16,0},{20,28},{24,8},{28,20},{1,17},{... | collective-permute-start | bytes 1769480 | tf_op jit(solution)/shard_map/ppermute | solution.py:168
  463.2 25.5 %collective-permute-start.83 = (bf16[96,768]{1,0:T(8,128)(2,1)S(1)}, bf16[96,768]{1,0:T(8,128)(2,1)S(1)}, u32[]{:S(2)}, u32[]{:S(2)}) collective-permute-start(bf16[96,768]{1,0:T(8,128)(2,1)S(1)} %get-tuple-element.79), channel_id=1, source_target_pairs={{0,1},{1,2},{2,3},{3,0},{4,5},{5,6},{6,7},{7,4},{8,9},{9,10},{10,1... | collective-permute-start | bytes 442376 | tf_op jit(solution)/shard_map/ppermute | solution.py:176
  463.3 25.5 %collective-permute-start.85 = (bf16[96,768]{1,0:T(8,128)(2,1)S(1)}, bf16[96,768]{1,0:T(8,128)(2,1)S(1)}, u32[]{:S(2)}, u32[]{:S(2)}) collective-permute-start(bf16[96,768]{1,0:T(8,128)(2,1)S(1)} %get-tuple-element.80), channel_id=1, source_target_pairs={{0,3},{1,0},{2,1},{3,2},{4,7},{5,4},{6,5},{7,6},{8,11},{9,8},{10,9... | collective-permute-start | bytes 442376 | tf_op jit(solution)/shard_map/ppermute | solution.py:176
  488.8 26.2 %collective-permute-start.56 = (bf16[4,96,576]{2,1,0:T(8,128)(2,1)S(1)}, bf16[4,96,576]{2,1,0:T(8,128)(2,1)S(1)}, u32[]{:S(2)}, u32[]{:S(2)}) collective-permute-start(bf16[4,96,576]{2,1,0:T(8,128)(2,1)S(1)} %dynamic-slice_bitcast_fusion.5), channel_id=1, source_target_pairs={{0,16},{4,12},{8,24},{12,4},{16,0},{20,28},{24,8},{28,20},{1,17},{... | collective-permute-start | bytes 1327112 | tf_op jit(solution)/shard_map/ppermute | solution.py:168
  (133 other events, 1240.9 us)

commit v2 on v0

v2 whole, which is shorter than its diff:
```python
import functools

import jax
import jax.numpy as jnp
from jax import lax
from jax.experimental import pallas as pl
from jax.experimental.pallas import tpu as pltpu
from jax.sharding import PartitionSpec as P

HEAD = 64
PLANE = 8
FACTOR = HEAD**-0.5 * 1.4426950408889634
BF = jnp.bfloat16
F32 = jnp.float32
NN = ((1,), (0,))
NT = ((1,), (1,))
TN = ((0,), (0,))
ATT, UP, DOWN = 0, 1, 2


def dot(left, right, dims):
    return lax.dot_general(left, right, (dims, ((), ())), preferred_element_type=F32)


def norm_parts(values):
    center = values - jnp.mean(values, axis=-1, keepdims=True)
    rate = lax.rsqrt(jnp.mean(center * center, axis=-1, keepdims=True) + 1e-5)
    return center * rate, rate


def norm_back(normed, rate, grad, gain):
    scaled = grad * gain
    mean = jnp.mean(scaled, axis=-1, keepdims=True)
    along = jnp.mean(scaled * normed, axis=-1, keepdims=True)
    return rate * (scaled - mean - normed * along)


def column_sum(values):
    return jnp.sum(values, axis=0, keepdims=True)


def layer_kernel(
    lines,
    whole_plane,
    tokens,
    cotangent,
    ids_in,
    shard_att,
    shard_up,
    shard_down,
    bias_in,
    vectors,
    block_home,
    input_home,
    grads_out,
    small_out,
    w,
    r_core,
    r_a,
    r_b,
    r_z,
    xb,
    gb,
    ids,
    bias,
    mask,
    n1,
    n2,
    n2t,
    middle,
    acc,
    acc2,
    dmr,
    qt,
    kv,
    kvs,
    kvg,
    ct,
    lse,
    bo,
    ig,
    sums,
    sums_z,
    sums_p,
    s_loc,
    s_ids,
    s_bias,
    s_x,
    s_g,
    s_bo,
    s_ig,
    s_kv,
    s_kvg,
    s_z,
    s_1,
    s_2,
    s_3,
    s_c,
    s_a,
    s_b,
    s_zg,
    s_g1,
    s_g2,
    s_g3,
    s_sz,
    s_sp,
):
    t = lax.axis_index("tensor")
    d = lax.axis_index("dp")
    e = lax.rem(d, PLANE)
    base = d - e
    c = lax.rem(e, 2)
    yx = e // 2
    x_bit = lax.rem(yx, 2)
    y_bit = yx // 2
    half = 512
    part = 192

    yx_x = 2 * y_bit + 1 - x_bit
    yx_y = 2 * (1 - y_bit) + x_bit
    yx_xy = 2 * (1 - y_bit) + 1 - x_bit
    yx_first = (1 - c) * yx_x + c * yx_y
    yx_second = (1 - c) * yx_y + c * yx_x

    def at(dp_index, line):
        return {"dp": dp_index, "tensor": line}

    dev_core = at(base + 2 * yx + 1 - c, t)
    dev_first = at(base + 2 * yx_first + c, t)
    dev_second = at(base + 2 * yx_second + c, t)

    def offset(s):
        return s + (s // 2) * (1 - 2 * (s % 2))

    def line_before(s):
        return at(d, lax.rem(t - offset(s) + lines, lines))

    def line_after(s):
        return at(d, lax.rem(t + offset(s), lines))

    def remote(src, dst, sems, dev):
        return pltpu.make_async_remote_copy(
            src_ref=src,
            dst_ref=dst,
            send_sem=sems[0],
            recv_sem=sems[1],
            device_id=dev,
            device_id_type=pl.DeviceIdType.MESH,
        )

    def pair(sem, *index):
        return sem.at[(0,) + index], sem.at[(1,) + index]

    barrier = pltpu.get_barrier_semaphore()
    for step in range(lines):
        for core in range(2):
            if step == 0 and core == 0:
                continue
            other = base + 2 * yx + lax.rem(c + core, 2)
            pl.semaphore_signal(
                barrier,
                1,
                device_id=at(other, lax.rem(t + step, lines)),
                device_id_type=pl.DeviceIdType.MESH,
            )
    for dev in (dev_first, dev_second):
        pl.semaphore_signal(barrier, 1, device_id=dev, device_id_type=pl.DeviceIdType.MESH)
    pl.semaphore_wait(barrier, 2 * lines - 1 + 2)

    def to_owner(src, dst, sem):
        for m in range(2):
            here = jnp.logical_and(t == 2 * c + m, c == t // 2)
            place = lax.rem(t, 2)
            dev = at(base + 2 * yx + t // 2, 2 * c + m)

            @pl.when(here)
            def _():
                pltpu.make_async_copy(src.at[m], dst.at[place], sem.at[1, place]).start()

            @pl.when(jnp.logical_not(here))
            def _():
                remote(src.at[m], dst.at[place], (sem.at[0, m], sem.at[1, place]), dev).start()

    def to_owner_wait(src, dst, sem):
        for k in range(2):
            pltpu.make_async_copy(dst.at[k], dst.at[k], sem.at[1, k]).wait()

    def to_owner_sent(src, sem):
        for m in range(2):
            here = jnp.logical_and(t == 2 * c + m, c == t // 2)

            @pl.when(jnp.logical_not(here))
            def _():
                remote(src.at[m], src.at[m], (sem.at[0, m], sem.at[1, m]), dev_core).wait_send()

    def to_home(src, dst, sem):
        to_owner(src, dst, sem)

    shards = (shard_att, shard_up, shard_down)

    def gather_z(i, s):
        return remote(
            shards[i].at[yx, c], w.at[i, s, yx, c], pair(s_z, i, s - 1), line_before(s)
        )

    def gather_1(i, s):
        ref = w.at[i, s, yx, c]
        return remote(ref, ref, pair(s_1, i, s - 1), dev_first)

    def gather_2(i, s, k):
        ref = w.at[i, s, yx if k == 0 else yx_first, c]
        return remote(ref, ref, pair(s_2, i, s - 1, k), dev_second)

    def gather_3(i, s):
        ref = w.at[i, s, :, c]
        return remote(ref, ref, pair(s_3, i, s - 1), dev_core)

    def step_1(i, s):
        gather_z(i, s).wait_recv()
        gather_1(i, s).start()

    def step_2(i, s):
        gather_1(i, s).wait_recv()
        gather_2(i, s, 0).start()
        gather_2(i, s, 1).start()

    def step_3(i, s):
        gather_2(i, s, 0).wait_recv()
        gather_2(i, s, 1).wait_recv()
        gather_3(i, s).start()

    def step_4(i, s):
        gather_3(i, s).wait()
        gather_1(i, s).wait_send()
        gather_2(i, s, 0).wait_send()
        gather_2(i, s, 1).wait_send()

    def add_into(dst, src):
        dst[...] = (dst[...].astype(F32) + src[...].astype(F32)).astype(BF)

    keep_other = yx_second
    send_k = [(1 - c) * (2 * k + 1 - x_bit) + c * (2 * (1 - y_bit) + k) for k in range(2)]
    keep_k = [(1 - c) * (2 * k + x_bit) + c * (2 * y_bit + k) for k in range(2)]
    k_mine = (1 - c) * y_bit + c * x_bit

    def reduce_core(i, s):
        return remote(w.at[i, s, :, 1 - c], r_core.at[i, s], pair(s_c, i, s), dev_core)

    def reduce_a(i, s, k):
        return remote(w.at[i, s, send_k[k], c], r_a.at[i, s, k], pair(s_a, i, s, k), dev_first)

    def reduce_b(i, s):
        return remote(w.at[i, s, keep_other, c], r_b.at[i, s], pair(s_b, i, s), dev_second)

    def reduce_z(i, s):
        return remote(w.at[i, s, yx, c], r_z.at[i, s - 1], pair(s_zg, i, s - 1), line_after(s))

    def fold_1(i, s):
        reduce_core(i, s).start()

    def fold_2(i, s):
        reduce_core(i, s).wait_recv()
        for k in range(2):
            add_into(w.at[i, s, send_k[k], c], r_core.at[i, s, send_k[k]])
            reduce_a(i, s, k).start()
        for k in range(2):
            add_into(w.at[i, s, keep_k[k], c], r_core.at[i, s, keep_k[k]])

    def fold_3(i, s):
        reduce_a(i, s, 0).wait_recv()
        reduce_a(i, s, 1).wait_recv()
        add_into(w.at[i, s, keep_other, c], r_a.at[i, s, 1 - k_mine])
        reduce_b(i, s).start()
        add_into(w.at[i, s, yx, c], r_a.at[i, s, k_mine])

    def fold_4(i, s):
        reduce_b(i, s).wait_recv()
        add_into(w.at[i, s, yx, c], r_b.at[i, s])
        if isinstance(s, int):
            if s > 0:
                reduce_z(i, s).start()
        else:

            @pl.when(s > 0)
            def _():
                reduce_z(i, s).start()

    def spread_1(i):
        ref = grads_out.at[i, yx, c]
        return remote(ref, ref, pair(s_g1, i), dev_first)

    def spread_2(i, k):
        ref = grads_out.at[i, yx if k == 0 else yx_first, c]
        return remote(ref, ref, pair(s_g2, i, k), dev_second)

    def spread_3(i):
        ref = grads_out.at[i, :, c]
        return remote(ref, ref, pair(s_g3, i), dev_core)

    def total(i):
        out = w[i, 0, yx, c].astype(F32)
        for s in range(1, lines):
            reduce_z(i, s).wait_recv()
            out = out + r_z[i, s - 1].astype(F32)
        if whole_plane:
            w[i, 0, yx, c] = out.astype(BF)
            copy = pltpu.make_async_copy(w.at[i, 0, yx, c], grads_out.at[i, yx, c], s_loc.at[3 + i])
        else:
            acc[pl.ds(96 * i, 96), :] = out
            copy = pltpu.make_async_copy(
                acc.at[pl.ds(96 * i, 96)], grads_out.at[i], s_loc.at[3 + i]
            )
        copy.start()
        copy.wait()
        if whole_plane:
            spread_1(i).start()

    def spread_step_2(i):
        if whole_plane:
            spread_1(i).wait_recv()
            spread_2(i, 0).start()
            spread_2(i, 1).start()

    def spread_step_3(i):
        if whole_plane:
            spread_2(i, 0).wait_recv()
            spread_2(i, 1).wait_recv()
            spread_3(i).start()

    ids_copy = remote(ids_in, ids.at[c], pair(s_ids), dev_core)
    ids_copy.start()
    bias_copies = [
        remote(bias_in, bias.at[s], pair(s_bias, s - 1), line_before(s)) for s in range(1, lines)
    ]
    for copy in bias_copies:
        copy.start()
    for s in range(1, lines):
        gather_z(ATT, s).start()
    to_owner(tokens, xb, s_x)
    own = [pltpu.make_async_copy(shards[i], w.at[i, 0], s_loc.at[i]) for i in range(3)]
    for copy in own:
        copy.start()
    bias[0] = bias_in[...]
    ids[pl.ds(c, 1)] = ids_in[...][None]

    remote(ids_in, ids.at[1 - c], pair(s_ids), dev_core).wait_recv()
    row = ids[t // 2, pl.ds(lax.rem(t, 2), 1), :].astype(F32)
    low, high = row[:, :half], row[:, half:]
    first_core = c == 0
    ids_own = jnp.where(first_core, low, high)
    ids_other = jnp.where(first_core, high, low)
    for place, ids_k in enumerate((ids_own, ids_other)):
        columns = jnp.broadcast_to(ids_k, (128, half)).T
        for j in range(0, half, 128):
            mask[place, :, j : j + 128] = jnp.where(columns == ids_own[:, j : j + 128], 0.0, -1e30)

    for s in range(1, lines):
        step_1(ATT, s)
    for s in range(1, lines):
        step_2(ATT, s)

    to_owner_wait(tokens, xb, s_x)
    for s in (1, 2):
        for i in (UP, DOWN):
            gather_z(i, s).start()
    normed, _ = norm_parts(xb[...].reshape(half, 768).astype(F32))
    n1[...] = (normed * vectors[0:1] + vectors[1:2]).astype(BF)
    for copy in bias_copies:
        copy.wait_recv()
    own[0].wait()

    def weights(i, s):
        return w[i, s].reshape(768, 768)

    def kv_copy(s):
        return remote(kv.at[s], kvs.at[s], pair(s_kv, s), dev_core)

    def project(s):
        qkv = dot(weights(ATT, s)[: 3 * part], n1[...], NT)
        bias_row = bias[s, 1:2, : 2 * part]
        bias_col = jnp.broadcast_to(bias_row, (128, 2 * part)).T[:, :1]
        qt[s] = (qkv[:part] + bias_col[:part]).astype(BF)
        kv[s, 0] = qkv[part : 2 * part].astype(BF)
        kv[s, 1] = (qkv[2 * part :] + bias_col[part:]).astype(BF)
        kv_copy(s).start()

    project(0)
    for s in range(1, lines):
        step_3(ATT, s)

    def attend(s, carry):
        @pl.when(s < lines - 1)
        def _():
            step_4(ATT, s + 1)
            project(s + 1)

        kv_copy(s).wait_recv()
        for h in range(part // HEAD):
            rows = slice(h * HEAD, (h + 1) * HEAD)
            q = qt[s, rows, :]
            s0 = dot(kv[s, 0, rows, :].T, q, NN) * FACTOR + mask[0]
            s1 = dot(kvs[s, 0, rows, :].T, q, NN) * FACTOR + mask[1]
            top = jnp.maximum(
                jnp.max(s0, axis=0, keepdims=True), jnp.max(s1, axis=0, keepdims=True)
            )
            p0 = jnp.exp2(s0 - top)
            p1 = jnp.exp2(s1 - top)
            weight = column_sum(p0) + column_sum(p1)
            out = dot(kv[s, 1, rows, :], p0.astype(BF), NN)
            out = out + dot(kvs[s, 1, rows, :], p1.astype(BF), NN)
            ct[s, rows, :] = (out / weight).astype(BF)
            lse[s, h : h + 1, :] = top + jnp.log2(weight)

        @pl.when(s == 0)
        def _():
            to_owner(cotangent, gb, s_g)

        @pl.when(s == 1)
        def _():
            step_1(UP, 1)
            step_1(DOWN, 1)

        @pl.when(s == 2)
        def _():
            step_2(UP, 1)
            step_2(DOWN, 1)
            step_1(UP, 2)
            step_1(DOWN, 2)
            gather_z(UP, 3).start()
            gather_z(DOWN, 3).start()

        @pl.when(s == 3)
        def _():
            step_3(UP, 1)
            step_3(DOWN, 1)
            step_2(UP, 2)
            step_2(DOWN, 2)

        return carry

    lax.fori_loop(0, lines, attend, 0)

    mid = xb[...].reshape(half, 768).astype(F32) + vectors[2:3]
    for s in range(lines):
        mid = mid + dot(ct[s], weights(ATT, s)[3 * part :], TN)
    middle[...] = mid
    normed, _ = norm_parts(mid)
    low_normed = (normed * vectors[3:4] + vectors[4:5]).astype(BF)
    n2[...] = low_normed
    n2t[...] = low_normed.T
    acc[...] = jnp.zeros_like(acc)
    acc2[...] = jnp.zeros_like(acc2)
    own[1].wait()
    own[2].wait()
    to_owner_wait(cotangent, gb, s_g)

    def feed(s, carry):
        @pl.when(s > 0)
        def _():
            step_4(UP, s)
            step_4(DOWN, s)

        grad = gb[...].reshape(half, 768)
        pre = dot(n2[...], weights(UP, s), NN) + bias[s, 0:1, :]
        phi = 0.5 * (1.0 + lax.erf(pre * 0.7071067811865476))
        active = (pre * phi).astype(BF)
        slope = phi + pre * jnp.exp(-0.5 * pre * pre) * 0.3989422804014327
        acc[...] += dot(active, weights(DOWN, s), NN)
        pre_grad = (dot(grad, weights(DOWN, s), NT) * slope).astype(BF)
        sums[s, 0:1, :] = column_sum(pre_grad.astype(F32))
        acc2[...] += dot(pre_grad, weights(UP, s), NT)
        w[DOWN, s] = dot(active, grad, TN).astype(BF).reshape(4, 2, 96, 768)
        fold_1(DOWN, s)
        w[UP, s] = dot(n2t[...], pre_grad, NN).astype(BF).reshape(4, 2, 96, 768)
        fold_1(UP, s)

        @pl.when(s == 0)
        def _():
            step_3(UP, 2)
            step_3(DOWN, 2)
            step_1(UP, 3)
            step_1(DOWN, 3)

        @pl.when(s == 1)
        def _():
            step_2(UP, 3)
            step_2(DOWN, 3)

        @pl.when(s == 2)
        def _():
            step_3(UP, 3)
            step_3(DOWN, 3)

        @pl.when(s >= 1)
        def _():
            fold_2(DOWN, s - 1)
            fold_2(UP, s - 1)

        @pl.when(s >= 2)
        def _():
            fold_3(DOWN, s - 2)
            fold_3(UP, s - 2)

        @pl.when(s >= 3)
        def _():
            fold_4(DOWN, s - 3)
            fold_4(UP, s - 3)

        return carry

    lax.fori_loop(0, lines, feed, 0)

    mid = middle[...]
    bo[...] = (mid + acc[...] + vectors[5:6]).astype(BF).reshape(2, 256, 768)
    to_home(bo, block_home, s_bo)
    normed, rate = norm_parts(mid)
    grad = gb[...].reshape(half, 768).astype(F32)
    back = acc2[...]
    middle_grad = grad + norm_back(normed, rate, back, vectors[3:4])
    vec_out = column_sum(middle_grad)
    vec_gain = column_sum(back * normed)
    vec_shift = column_sum(back)
    vec_down = column_sum(grad)
    for s in range(lines):
        sums[s, 4:5, :] = vec_out
        sums[s, 5:6, :] = vec_gain
        sums[s, 6:7, :] = vec_shift
        sums[s, 7:8, :] = vec_down
    acc2[...] = middle_grad
    dmr[...] = middle_grad.astype(BF)
    acc[...] = jnp.zeros_like(acc)

    def kvg_copy(s):
        return remote(kvs.at[s], kvg.at[s], pair(s_kvg, s), dev_core)

    def finish(s):
        kvg_copy(s).wait_recv()
        dq = qt[s]
        dkv = (kv[s].astype(F32) + kvg[s].astype(F32)).astype(BF).reshape(2 * part, half)
        ones = jnp.ones((8, half), BF)
        sums[s, 1:2, :part] = dot(ones, dq, NT)[:1]
        sums[s, 1:2, part : 2 * part] = dot(ones, dkv[part:], NT)[:1]
        sums[s, 1:2, 2 * part :] = jnp.zeros((1, 768 - 2 * part), F32)
        stacked = jnp.concatenate([dq, dkv], axis=0)
        acc[...] += dot(stacked, weights(ATT, s)[: 3 * part], TN)
        w[ATT, s, 0:3] = dot(stacked, n1[...], NN).astype(BF).reshape(3, 2, 96, 768)
        fold_1(ATT, s)

    def attend_back(s, carry):
        dct = dot(w[ATT, s, 3].reshape(part, 768), dmr[...], NT).astype(BF)
        w[ATT, s, 3] = dot(ct[s], dmr[...], NN).astype(BF).reshape(2, 96, 768)
        kv_copy(s).wait_send()
        for h in range(part // HEAD):
            rows = slice(h * HEAD, (h + 1) * HEAD)
            g = dct[rows]
            q = qt[s, rows, :]
            along = column_sum(g.astype(F32) * ct[s, rows, :].astype(F32))
            total_log = lse[s, h : h + 1, :]
            dq = jnp.zeros((HEAD, half), F32)
            for place, ref in enumerate((kv, kvs)):
                k = ref[s, 0, rows, :]
                v = ref[s, 1, rows, :]
                p = jnp.exp2(dot(k.T, q, NN) * FACTOR + mask[place] - total_log)
                ds = (p * (dot(v.T, g, NN) - along)).astype(BF)
                ref[s, 0, rows, :] = (dot(q, ds, NT) * HEAD**-0.5).astype(BF)
                ref[s, 1, rows, :] = dot(g, p.astype(BF), NT).astype(BF)
                dq = dq + dot(k, ds, NN)
            qt[s, rows, :] = (dq * HEAD**-0.5).astype(BF)
        kvg_copy(s).start()

        @pl.when(s == 0)
        def _():
            for i in (DOWN, UP):
                fold_2(i, 3)
                fold_3(i, 2)
                fold_4(i, 1)

        @pl.when(s == 1)
        def _():
            for i in (DOWN, UP):
                fold_3(i, 3)
                fold_4(i, 2)

        @pl.when(s == 2)
        def _():
            for i in (DOWN, UP):
                fold_4(i, 3)
            fold_2(ATT, 0)

        @pl.when(s == 3)
        def _():
            total(DOWN)
            total(UP)
            fold_2(ATT, 1)
            fold_3(ATT, 0)

        @pl.when(s > 0)
        def _():
            finish(s - 1)

        return carry

    lax.fori_loop(0, lines, attend_back, 0)
    finish(3)

    normed, rate = norm_parts(xb[...].reshape(half, 768).astype(F32))
    back = acc[...]
    ig[...] = (
        (acc2[...] + norm_back(normed, rate, back, vectors[0:1])).astype(BF).reshape(2, 256, 768)
    )
    to_home(ig, input_home, s_ig)
    vec_gain = column_sum(back * normed)
    vec_shift = column_sum(back)
    for s in range(lines):
        sums[s, 2:3, :] = vec_gain
        sums[s, 3:4, :] = vec_shift

    def sums_copy(s):
        return remote(sums.at[s], sums_z.at[t], pair(s_sz, s - 1), line_after(s))

    for s in range(1, lines):
        sums_copy(s).start()
    sums_z[pl.ds(t, 1)] = sums[0:1]

    fold_2(ATT, 2)
    fold_3(ATT, 1)
    fold_4(ATT, 0)
    spread_step_2(DOWN)
    spread_step_2(UP)
    fold_2(ATT, 3)
    fold_3(ATT, 2)
    fold_4(ATT, 1)
    for s in range(1, lines):
        sums_copy(s).wait()
    sums_p[0] = (sums_z[0] + sums_z[1]) + (sums_z[2] + sums_z[3])

    dev_x = at(base + 2 * yx_x + c, t)
    dev_y = at(base + 2 * yx_y + c, t)

    def flip(k):
        return remote(
            sums_p.at[2 * k], sums_p.at[2 * k + 1], pair(s_sp, k), (dev_core, dev_x, dev_y)[k]
        )

    flip(0).start()
    spread_step_3(DOWN)
    spread_step_3(UP)
    fold_3(ATT, 3)
    fold_4(ATT, 2)
    flip(0).wait()
    sums_p[2] = sums_p[0] + sums_p[1]
    flip(1).start()
    fold_4(ATT, 3)
    flip(1).wait()
    sums_p[4] = sums_p[2] + sums_p[3]
    flip(2).start()
    total(ATT)
    flip(2).wait()
    small_out[...] = sums_p[4] + sums_p[5]
    spread_step_2(ATT)
    spread_step_3(ATT)

    ids_copy.wait_send()
    for copy in bias_copies:
        copy.wait_send()
    to_owner_sent(tokens, s_x)
    to_owner_sent(cotangent, s_g)
    to_owner_wait(bo, block_home, s_bo)
    to_owner_sent(bo, s_bo)
    to_owner_wait(ig, input_home, s_ig)
    to_owner_sent(ig, s_ig)
    for i in range(3):
        for s in range(1, lines):
            gather_z(i, s).wait_send()
            reduce_z(i, s).wait_send()
        for s in range(lines):
            reduce_core(i, s).wait_send()
            reduce_a(i, s, 0).wait_send()
            reduce_a(i, s, 1).wait_send()
            reduce_b(i, s).wait_send()
        if whole_plane:
            spread_1(i).wait_send()
            spread_2(i, 0).wait_send()
            spread_2(i, 1).wait_send()
            spread_3(i).wait()
    for s in range(lines):
        kvg_copy(s).wait_send()


def layer(lines, whole_plane, operands):
    def dma(*shape):
        return pltpu.SemaphoreType.DMA((2,) + shape)

    def vmem(*shape, dtype=BF):
        return pltpu.VMEM(shape, dtype)

    n = lines
    anywhere = pl.BlockSpec(memory_space=pl.ANY)
    inside = pl.BlockSpec(memory_space=pltpu.VMEM)
    piece = (96, 768)
    if whole_plane:
        grads = jax.ShapeDtypeStruct((3, 4, 2) + piece, BF)
    else:
        grads = jax.ShapeDtypeStruct((3,) + piece, F32)
    blocks = jax.ShapeDtypeStruct((2, 256, 768), BF)
    return pl.pallas_call(
        functools.partial(layer_kernel, lines, whole_plane),
        in_specs=[anywhere, anywhere, inside, anywhere, anywhere, anywhere, inside, inside],
        out_specs=[anywhere, anywhere, anywhere, inside],
        out_shape=[blocks, blocks, grads, jax.ShapeDtypeStruct((8, 768), F32)],
        scratch_shapes=[
            vmem(3, n, 4, 2, *piece),
            vmem(3, n, 4, *piece),
            vmem(3, n, 2, *piece),
            vmem(3, n, *piece),
            vmem(3, n - 1, *piece),
            vmem(2, 256, 768),
            vmem(2, 256, 768),
            vmem(2, 2, 1024, dtype=jnp.int32),
            vmem(n, 8, 768, dtype=F32),
            vmem(2, 512, 512, dtype=F32),
            vmem(512, 768),
            vmem(512, 768),
            vmem(768, 512),
            vmem(512, 768, dtype=F32),
            vmem(512, 768, dtype=F32),
            vmem(512, 768, dtype=F32),
            vmem(512, 768),
            vmem(n, 192, 512),
            vmem(n, 2, 192, 512),
            vmem(n, 2, 192, 512),
            vmem(n, 2, 192, 512),
            vmem(n, 192, 512),
            vmem(n, 8, 512, dtype=F32),
            vmem(2, 256, 768),
            vmem(2, 256, 768),
            vmem(n, 8, 768, dtype=F32),
            vmem(n, 8, 768, dtype=F32),
            vmem(6, 8, 768, dtype=F32),
            pltpu.SemaphoreType.DMA((6,)),
            dma(),
            dma(n - 1),
            dma(2),
            dma(2),
            dma(2),
            dma(2),
            dma(n),
            dma(n),
            dma(3, n - 1),
            dma(3, n - 1),
            dma(3, n - 1, 2),
            dma(3, n - 1),
            dma(3, n),
            dma(3, n, 2),
            dma(3, n),
            dma(3, n - 1),
            dma(3),
            dma(3, 2),
            dma(3),
            dma(n - 1),
            dma(3),
        ],
        compiler_params=pltpu.CompilerParams(
            collective_id=0, has_side_effects=True, vmem_limit_bytes=62 * 2**20
        ),
        name="layer",
    )(*operands)


def body(
    dp,
    lines,
    tokens,
    segment_ids,
    gain_first,
    shift_first,
    weight_qkv,
    bias_qv,
    weight_out,
    bias_out,
    gain_second,
    shift_second,
    weight_up,
    bias_up,
    weight_down,
    bias_down,
    cotangent,
):
    width = tokens.shape[2]
    part = weight_qkv.shape[2]
    shard = (4, 2, width // PLANE, width)
    att = jnp.concatenate([weight_qkv.reshape(width, 3 * part).T, weight_out], axis=0)
    low = jnp.concatenate([bias_qv.reshape(-1), jnp.zeros((width - 2 * part,), F32)])
    bias = jnp.concatenate([bias_up[None], low[None], jnp.zeros((6, width), F32)])
    zero = jnp.zeros((width,), F32)
    vectors = jnp.stack(
        [gain_first, shift_first, bias_out, gain_second, shift_second, bias_down, zero, zero]
    )
    whole_plane = dp == PLANE
    block_out, input_grad, grads, small = layer(
        lines,
        whole_plane,
        (
            tokens,
            cotangent,
            segment_ids,
            att.reshape(shard),
            weight_up.reshape(shard),
            weight_down.reshape(shard),
            bias,
            vectors,
        ),
    )
    if not whole_plane:
        apart = [[i + PLANE * g for g in range(dp // PLANE)] for i in range(PLANE)]
        planes = [[i + PLANE * g for i in range(PLANE)] for g in range(dp // PLANE)]
        grads, small = lax.psum((grads, small), "dp", axis_index_groups=apart)
        grads = lax.all_gather(grads.astype(BF), "dp", axis=1, axis_index_groups=planes)
    grads = grads.reshape(3, width, width).astype(F32)
    att_grad = grads[0]
    return (
        block_out,
        input_grad.astype(F32),
        small[2],
        small[3],
        att_grad[: 3 * part].T.reshape(width, 3, part),
        small[1, : 2 * part].reshape(2, part),
        att_grad[3 * part :],
        small[4],
        small[5],
        small[6],
        grads[1],
        small[0],
        grads[2],
        small[7],
    )


def solution(mesh):
    in_specs = (
        P("dp", "tensor", None),
        P("dp", None),
        P(),
        P(),
        P(None, None, "tensor"),
        P(None, "tensor"),
        P("tensor", None),
        P(),
        P(),
        P(),
        P(None, "tensor"),
        P("tensor"),
        P("tensor", None),
        P(),
        P("dp", "tensor", None),
    )
    out_specs = (
        P("dp", "tensor", None),
        P("dp", "tensor", None),
        P(),
        P(),
        P(None, None, "tensor"),
        P(None, "tensor"),
        P("tensor", None),
        P(),
        P(),
        P(),
        P(None, "tensor"),
        P("tensor"),
        P("tensor", None),
        P(),
    )
    whole = functools.partial(body, mesh.shape["dp"], mesh.shape["tensor"])
    return jax.shard_map(whole, mesh=mesh, in_specs=in_specs, out_specs=out_specs, check_vma=False)
```

time: 847 us -> 224 us (0.26)
  waiting for transfers between devices: 499 us -> 0 us
  Pallas kernels: 0 us -> 205 us
  matrix products: 152 us -> 0 us
  other arithmetic: 70.7 us -> 7.17 us
  blocking collectives: 54.5 us -> 0 us
  loops' own time: 26.6 us -> 0 us
  between operations: 15.5 us -> 0.85 us
  local copies, waits for them, and re-layouts: 24.7 us -> 10.4 us
    all_gather x8 -> x0, waiting for transfers between devices: 257 us -> none  [the longest x2 70.5 us: run_forward(): sent_second = lax.all_gather(normed_second, 'tensor', axis=0, tiled=True)]
    pallas_call x0 -> x1, Pallas kernels: none -> 205 us  [layer(): pl.pallas_call(functools.partial(layer_kernel, lines, whole_plane), in_sp...]
    reduce_scatter x8 -> x0, waiting for transfers between devices: 178 us -> none  [the longest x2 68.5 us: run_forward(): lax.psum_scatter(jnp.dot(context, weight_out, preferred_element_type=jnp....]
    dot_general x36 -> x0, matrix products: 152 us -> none  [the longest x8 30.4 us: contract_rows(): lax.dot_general(left, right, (((0,), (0,)), ((), ())), preferred_element_...]
    psum x1 -> x0, waiting for transfers between devices: 63.4 us -> none  [body(): lax.psum((grads[0], grads[1], grads[2], grads[3], grads[4], grads[5]), 'dp')]
    psum x2 -> x0, blocking collectives: 54.5 us -> none  [the longest x1 40.1 us: body(): lax.psum((sums[0], sums[1], sums[2], sums[3], sums[4], sums[5]), ('dp', '...]
    reduce_sum x22 -> x0, other arithmetic: 35 us -> none  [the longest x2 8.76 us: run_forward(): log_totals = jax.nn.logsumexp(scores, axis=-1, keepdims=True)]
    another operation x1 -> x0, loops' own time: 26.6 us -> none  [body(): lax.scan(micro_step, (zero_grads, zero_sums), (tokens, segment_ids, cotan...]
  transfers between devices with their start and end apart: 17 -> 0, of which waited for: 15 -> 0; matrix products, arithmetic and copies ran while one was open for 16% -> 0% of each run, Pallas kernels for 0% -> 0%
where the time goes in v2:
time: 224 us; the launch traced here: 223 us
  Pallas kernels  205 us (92%)
  local copies, waits for them, and re-layouts  10.4 us (5%)
  other arithmetic  7.17 us (3%)
    pallas_call x1, Pallas kernels, layer(): pl.pallas_call(functools.partial(layer_kernel, lines, whole_plane), in_sp...  205 us

profile of v2, /device:TPU:0, one launch (start us, length us, event | category | flops | bytes accessed | tf_op | source)
XLA Modules:
  0.0 223.2 jit_solution(6694126861706842992)
XLA Ops:
  0.6 0.0 copy-start.3
  0.7 0.0 copy-start.4
  0.7 0.0 copy-start.5
  0.7 0.0 copy-start.6
  0.7 0.0 copy-start.7
  0.7 0.0 copy-start.8
  0.7 0.0 copy-start.10
  0.7 0.0 copy-start.9
  0.7 2.4 %pad_maximum_fusion = bf16[768,768]{1,0:T(8,128)(2,1)} fusion(bf16[192,768]{1,0:T(8,128)(2,1)} %param.21, bf16[576,768]{1,0:T(8,128)(2,1)} %bitcast.24), kind=kLoop, calls=%fused_computation | loop fusion | flops 2359296 | bytes 2359296 | tf_op jit(solution)/shard_map/concatenate | solution.py:792
  3.1 0.0 copy-done.3
  3.1 0.0 copy-done.4
  3.1 0.0 copy-done.5
  3.2 0.0 copy-done.6
  3.2 0.0 copy-done.7
  3.2 0.0 copy-done.8
  3.2 0.6 stack.31.vectors
  3.9 0.0 copy-done.10
  3.9 0.1 reshape.58
  4.0 0.0 copy-done.9
  4.0 0.1 pad.3.clone
  4.1 0.7 maximum_maximum_fusion.bias_in
  4.8 204.8 %layer.1 = (bf16[2,256,768]{2,1,0:T(8,128)(2,1)}, bf16[2,256,768]{2,1,0:T(8,128)(2,1)}, bf16[3,4,2,96,768]{4,3,2,1,0:T(8,128)(2,1)}, f32[8,768]{1,0:T(8,128)}) custom-call(bf16[2,256,768]{2,1,0:T(8,128)(2,1)} %tokens.1, bf16[2,256,768]{2,1,0:T(8,128)(2,1)} %cotangent.1, s32[2,1024]{1,0:T(2,128)} %ids_in.1, bf16[4,2,96,768]{3,2,1,0:T(8,128)(2,1)} %bitcast.18, ...), custom_call_target="tpu_custom_call" | custom-call | tf_op jit(solution)/shard_map/layer/pallas_call | solution.py:706
  209.5 1.7 slice_reduce_fusion
  211.2 2.8 %convert_element_type.10 = f32[3,4,2,96,768]{4,3,2,1,0:T(8,128)S(1)} convert(bf16[3,4,2,96,768]{4,3,2,1,0:T(8,128)(2,1)} %get-tuple-element.21) | non-fusion elementwise | flops 1769472 | bytes 10616832 | tf_op jit(solution)/shard_map/convert_element_type | solution.py:819
  214.1 1.3 slice.61
  215.4 0.9 slice_bitcast_fusion
  216.3 0.7 copy-done
  216.9 2.7 %fusion = (f32[1,4,2,96,768]{4,3,2,1,0:T(8,128)}, f32[1,4,2,96,768]{4,3,2,1,0:T(8,128)}) fusion(bf16[3,4,2,96,768]{4,3,2,1,0:T(8,128)(2,1)S(1)} %copy-done), kind=kLoop, calls=%fused_computation.11 | loop fusion | bytes 9437184 | tf_op jit(solution)/shard_map/slice | solution.py:834
  219.6 0.8 slice_reduce_fusion.7
  220.4 0.7 reshape_squeeze.3
  221.1 1.3 convert_element_type.9
  222.3 0.9 copy.30
  (16 shorter events, 0.1 us)
Async XLA Ops:
  0.6 2.5 %copy-start.3 = (f32[768]{0:T(1024)S(1)}, f32[768]{0:T(1024)}, u32[]{:S(2)}) copy-start(f32[768]{0:T(1024)} %param.17) | copy-start | bytes 9220
  0.7 2.5 %copy-start.4 = (f32[768]{0:T(1024)S(1)}, f32[768]{0:T(1024)}, u32[]{:S(2)}) copy-start(f32[768]{0:T(1024)} %param.18) | copy-start | bytes 9220
  0.7 2.5 %copy-start.5 = (f32[768]{0:T(1024)S(1)}, f32[768]{0:T(1024)}, u32[]{:S(2)}) copy-start(f32[768]{0:T(1024)} %param.22) | copy-start | bytes 9220
  0.7 2.5 %copy-start.6 = (f32[768]{0:T(1024)S(1)}, f32[768]{0:T(1024)}, u32[]{:S(2)}) copy-start(f32[768]{0:T(1024)} %param.23) | copy-start | bytes 9220
  0.7 2.5 %copy-start.7 = (f32[768]{0:T(1024)S(1)}, f32[768]{0:T(1024)}, u32[]{:S(2)}) copy-start(f32[768]{0:T(1024)} %param.24) | copy-start | bytes 9220
  0.7 2.5 %copy-start.8 = (f32[768]{0:T(1024)S(1)}, f32[768]{0:T(1024)}, u32[]{:S(2)}) copy-start(f32[768]{0:T(1024)} %param.28) | copy-start | bytes 9220
  0.7 3.2 %copy-start.10 = (f32[2,192]{1,0:T(2,128)S(1)}, f32[2,192]{1,0:T(2,128)}, u32[]{:S(2)}) copy-start(f32[2,192]{1,0:T(2,128)} %param.20) | copy-start | bytes 4612
  0.7 3.3 %copy-start.9 = (f32[768]{0:T(1024)S(1)}, f32[768]{0:T(1024)}, u32[]{:S(2)}) copy-start(f32[768]{0:T(1024)} %param.26) | copy-start | bytes 9220
  214.1 2.9 %copy-start = (bf16[3,4,2,96,768]{4,3,2,1,0:T(8,128)(2,1)S(1)}, bf16[3,4,2,96,768]{4,3,2,1,0:T(8,128)(2,1)}, u32[]{:S(2)}) copy-start(bf16[3,4,2,96,768]{4,3,2,1,0:T(8,128)(2,1)} %get-tuple-element.21) | copy-start | bytes 10616836
  216.9 4.2 %copy-start.2 = (bf16[2,256,768]{2,1,0:T(8,128)(2,1)S(1)}, bf16[2,256,768]{2,1,0:T(8,128)(2,1)}, u32[]{:S(2)}) copy-start(bf16[2,256,768]{2,1,0:T(8,128)(2,1)} %get-tuple-element.19) | copy-start | bytes 2359300
  219.6 2.7 %copy-start.1 = (bf16[2,256,768]{2,1,0:T(8,128)(2,1)S(1)}, bf16[2,256,768]{2,1,0:T(8,128)(2,1)}, u32[]{:S(2)}) copy-start(bf16[2,256,768]{2,1,0:T(8,128)(2,1)} %get-tuple-element.45) | copy-start | bytes 2359300

commit v3 on v2

v3 whole, which is shorter than its diff:
```python
import functools

import jax
import jax.numpy as jnp
from jax import lax
from jax.experimental import pallas as pl
from jax.experimental.pallas import tpu as pltpu
from jax.sharding import PartitionSpec as P

HEAD = 64
PLANE = 8
FACTOR = HEAD**-0.5 * 1.4426950408889634
BF = jnp.bfloat16
F32 = jnp.float32
NN = ((1,), (0,))
NT = ((1,), (1,))
TN = ((0,), (0,))
ATT, FFN = 0, 1

Z_OWN, Z_PASS, STEP_1, STEP_2, STEP_3, FOLD_2, FOLD_3, FOLD_4, FOLD_5, TOTAL = range(10)
SPREAD_2, SPREAD_3, FINISH, SEE, SUMS, SUMS_Z, SUMS_P, SUMS_END, MOVE = range(10, 19)
X, G, BO, IG = range(4)
START, X_HERE, FIRST, ATTEND, OUT, FEED, BLOCK, NORM, BACK, TAIL_0, TAIL_1, TAIL_2, TAIL_3 = range(13)

ORDER = (3, 2, 1, 0)

PLAN = {
    (START,): (
        (Z_OWN, ATT),
        (Z_OWN, FFN),
        (Z_PASS, ATT, 1),
        (MOVE, X, 0, 0),
        (Z_PASS, FFN, 1),
        (STEP_1, ATT, 1),
        (MOVE, X, 1, 1),
        (Z_PASS, ATT, 2),
        (STEP_1, FFN, 1),
        (MOVE, X, 0, 1),
        (STEP_2, ATT, 1),
        (STEP_1, ATT, 2),
        (SEE,),
        (Z_PASS, FFN, 2),
        (MOVE, X, 1, 0),
        (STEP_2, ATT, 2),
        (STEP_2, FFN, 1),
        (Z_PASS, ATT, 3),
    ),
    (X_HERE,): (
        (MOVE, G, 0, 1),
        (STEP_3, ATT, 1),
        (STEP_1, ATT, 3),
    ),
    (FIRST,): (
        (STEP_1, FFN, 2),
    ),
    (ATTEND, 0, 0): (
        (STEP_3, ATT, 2),
    ),
    (ATTEND, 0, 1): (
        (STEP_2, ATT, 3),
    ),
    (ATTEND, 0, 2): (
        (Z_PASS, FFN, 3),
        (MOVE, G, 0, 0),
        (MOVE, G, 1, 0),
    ),
    (ATTEND, 1, 1): (
        (STEP_2, FFN, 2),
        (MOVE, G, 1, 1),
    ),
    (ATTEND, 1, 2): (
        (STEP_3, ATT, 3),
    ),
    (ATTEND, 2, 0): (
        (STEP_3, FFN, 1),
    ),
    (ATTEND, 3, 0): (
        (STEP_1, FFN, 3),
    ),
    (OUT,): (
        (STEP_3, FFN, 2),
    ),
    (FEED, 0, 2): (
        (STEP_2, FFN, 3),
    ),
    (FEED, 1, 5): (
        (FOLD_2, FFN, 0),
        (STEP_3, FFN, 3),
    ),
    (FEED, 2, 5): (
        (FOLD_2, FFN, 1),
    ),
    (BLOCK,): (
        (MOVE, BO, 0, 0),
        (MOVE, BO, 1, 1),
    ),
    (NORM,): (
        (MOVE, BO, 1, 0),
    ),
    (BACK, 0, 0): (
        (FOLD_2, FFN, 2),
    ),
    (BACK, 1, 0): (
        (FOLD_2, FFN, 3),
        (FINISH, 3),
    ),
    (BACK, 1, 2): (
        (FOLD_2, ATT, 3),
    ),
    (BACK, 1, 3): (
        (MOVE, BO, 0, 1),
        (FOLD_3, FFN, 3),
        (FOLD_3, FFN, 2),
        (FINISH, 2),
    ),
    (BACK, 2, 0): (
        (FOLD_4, FFN, 3),
        (FOLD_3, ATT, 3),
    ),
    (BACK, 2, 3): (
        (FOLD_2, ATT, 2),
        (FOLD_4, ATT, 3),
        (FOLD_3, FFN, 1),
    ),
    (BACK, 3, 0): (
        (FOLD_5, FFN, 3),
        (FOLD_4, FFN, 2),
        (FOLD_3, FFN, 0),
    ),
    (BACK, 3, 1): (
        (FINISH, 1),
        (FOLD_5, ATT, 3),
    ),
    (BACK, 3, 2): (
        (FOLD_3, ATT, 2),
    ),
    (BACK, 3, 3): (
        (FOLD_4, FFN, 1),
        (FOLD_5, FFN, 1),
        (FOLD_2, ATT, 1),
    ),
    (TAIL_0,): (
        (FOLD_5, FFN, 2),
        (FINISH, 0),
        (FOLD_4, FFN, 0),
    ),
    (TAIL_2,): (
        (SUMS,),
        (FOLD_4, ATT, 2),
        (MOVE, IG, 1, 1),
        (FOLD_3, ATT, 1),
        (FOLD_2, ATT, 0),
        (TOTAL, FFN),
    ),
    (TAIL_3,): (
        (FOLD_4, ATT, 1),
        (FOLD_5, ATT, 2),
        (MOVE, IG, 0, 1),
        (FOLD_5, ATT, 1),
        (SUMS_Z,),
        (MOVE, IG, 0, 0),
        (FOLD_3, ATT, 0),
        (MOVE, IG, 1, 0),
        (SPREAD_2, FFN),
        (SUMS_P, 1),
        (FOLD_4, ATT, 0),
        (TOTAL, ATT),
        (SPREAD_2, ATT),
        (SPREAD_3, FFN),
        (SPREAD_3, ATT),
        (SUMS_P, 2),
        (SUMS_END,),
    ),
}


def dot(left, right, dims):
    return lax.dot_general(left, right, (dims, ((), ())), preferred_element_type=F32)


def norm_parts(values):
    center = values - jnp.mean(values, axis=-1, keepdims=True)
    rate = lax.rsqrt(jnp.mean(center * center, axis=-1, keepdims=True) + 1e-5)
    return center * rate, rate


def norm_back(normed, rate, grad, gain):
    scaled = grad * gain
    mean = jnp.mean(scaled, axis=-1, keepdims=True)
    along = jnp.mean(scaled * normed, axis=-1, keepdims=True)
    return rate * (scaled - mean - normed * along)


def column_sum(values):
    return jnp.sum(values, axis=0, keepdims=True)


def layer_kernel(
    lines,
    whole_plane,
    tokens,
    cotangent,
    ids_in,
    shard_qkv,
    shard_out,
    shard_up,
    shard_down,
    bias_up,
    bias_qv,
    gain_first,
    shift_first,
    bias_out,
    gain_second,
    shift_second,
    bias_down,
    block_home,
    input_home,
    grads_att,
    grads_up,
    grads_down,
    small_out,
    w_att,
    w_ffn,
    r_core_att,
    r_core_ffn,
    r_a_att,
    r_a_ffn,
    r_b_att,
    r_b_ffn,
    r_z_att,
    r_z_ffn,
    xb,
    gb,
    ids,
    bias,
    mask,
    n1,
    n2,
    n2t,
    middle,
    acc,
    acc2,
    dmr,
    qt,
    kv,
    kvs,
    kvg,
    ct,
    lse,
    bo,
    ig,
    sums,
    sums_z,
    sums_p,
    s_loc,
    s_ids,
    s_bias,
    s_x,
    s_g,
    s_bo,
    s_ig,
    s_kv,
    s_kvg,
    s_zs,
    s_zr,
    s_1,
    s_2,
    s_3,
    s_c,
    s_a,
    s_b,
    s_zgs,
    s_zgr,
    s_g1,
    s_g2,
    s_g3,
    s_sz,
    s_sp,
):
    t = lax.axis_index("tensor")
    d = lax.axis_index("dp")
    e = lax.rem(d, PLANE)
    base = d - e
    c = lax.rem(e, 2)
    yx = e // 2
    x_bit = lax.rem(yx, 2)
    y_bit = yx // 2
    half = 512
    part = 192
    width = 768
    w_of = (w_att, w_ffn)
    r_core = (r_core_att, r_core_ffn)
    r_a = (r_a_att, r_a_ffn)
    r_b = (r_b_att, r_b_ffn)
    r_z = (r_z_att, r_z_ffn)
    grads_out = ((grads_att,), (grads_up, grads_down))
    gain_first, shift_first, bias_out = [r[...][None] for r in (gain_first, shift_first, bias_out)]
    gain_second, shift_second = gain_second[...][None], shift_second[...][None]
    bias_down = bias_down[...][None]

    yx_x = 2 * y_bit + 1 - x_bit
    yx_y = 2 * (1 - y_bit) + x_bit
    yx_first = (1 - c) * yx_x + c * yx_y
    yx_second = (1 - c) * yx_y + c * yx_x

    def at(dp_index, line):
        return {"dp": dp_index, "tensor": line}

    dev_core = at(base + 2 * yx + 1 - c, t)
    dev_first = at(base + 2 * yx_first + c, t)
    dev_second = at(base + 2 * yx_second + c, t)

    def by_line_of(place, *values):
        out = values[3]
        for k in (2, 1, 0):
            out = jnp.where(place == k, values[k], out)
        return out

    def by_line(*values):
        return by_line_of(t, *values)

    source = [t, by_line(1, 2, 3, 2), by_line(2, 0, 1, 1), by_line(3, 3, 0, 0)]
    inner = jnp.logical_and(t > 0, t < lines - 1)
    outer = jnp.logical_not(inner)

    def remote(src, dst, sems, dev):
        return pltpu.make_async_remote_copy(
            src_ref=src,
            dst_ref=dst,
            send_sem=sems[0],
            recv_sem=sems[1],
            device_id=dev,
            device_id_type=pl.DeviceIdType.MESH,
        )

    def pair(sem, *index):
        return sem.at[(0,) + index], sem.at[(1,) + index]

    barrier = pltpu.get_barrier_semaphore()
    for step in range(lines):
        for core in range(2):
            if step == 0 and core == 0:
                continue
            other = base + 2 * yx + lax.rem(c + core, 2)
            pl.semaphore_signal(
                barrier,
                1,
                device_id=at(other, lax.rem(t + step, lines)),
                device_id_type=pl.DeviceIdType.MESH,
            )
    for dev in (dev_first, dev_second):
        pl.semaphore_signal(barrier, 1, device_id=dev, device_id_type=pl.DeviceIdType.MESH)
    pl.semaphore_wait(barrier, 2 * lines - 1 + 2)

    def to_owner(src, dst, sem, m, h):
        here = jnp.logical_and(t == 2 * c + m, c == t // 2)
        place = lax.rem(t, 2)
        dev = at(base + 2 * yx + t // 2, 2 * c + m)
        rows = pl.ds(128 * h, 128)
        out, into = src.at[m, rows], dst.at[place, rows]

        @pl.when(here)
        def _():
            pltpu.make_async_copy(out, into, sem.at[1, place, h]).start()

        @pl.when(jnp.logical_not(here))
        def _():
            remote(out, into, (sem.at[0, m, h], sem.at[1, place, h]), dev).start()

    def to_owner_wait(src, dst, sem):
        for k in range(2):
            for h in range(2):
                ref = dst.at[k, pl.ds(128 * h, 128)]
                pltpu.make_async_copy(ref, ref, sem.at[1, k, h]).wait()

    def to_owner_sent(src, sem):
        for m in range(2):
            here = jnp.logical_and(t == 2 * c + m, c == t // 2)

            @pl.when(jnp.logical_not(here))
            def _():
                for h in range(2):
                    ref = src.at[m, pl.ds(128 * h, 128)]
                    remote(ref, ref, (sem.at[0, m, h], sem.at[1, m, h]), dev_core).wait_send()

    def piece(i, s, place):
        return w_of[i].at[s, place, c]

    def z_right(i, src):
        slot = 2 - t // 2
        return remote(
            src, w_of[i].at[slot, yx, c], (s_zs.at[i, 0], s_zr.at[i, slot]), at(d, t + 1)
        )

    def z_left(i, src):
        return remote(src, w_of[i].at[1, yx, c], (s_zs.at[i, 1], s_zr.at[i, 1]), at(d, t - 1))

    def z_own(i):
        for copy in own[2 * i : 2 * i + 2]:
            copy.wait()
        pl.when(t < lines - 1)(lambda: z_right(i, own_piece[i]).start())
        pl.when(t > 0)(lambda: z_left(i, own_piece[i]).start())

    def z_forward(i, s):
        slot = (0, t + 1, 4 - t, 3)[s]
        line = (0, t - 1, t + 1, 3 * t - 3)[s]
        src = piece(i, s, yx)
        return remote(
            src, w_of[i].at[slot, yx, c], (s_zs.at[i, 1 + s], s_zr.at[i, slot]), at(d, line)
        )

    def z_got(i, s):
        ref = piece(i, s, yx)
        remote(ref, ref, (s_zs.at[i, 1 + s], s_zr.at[i, s]), dev_core).wait_recv()

    def z_pass(i, s):
        @pl.when(inner)
        def _():
            z_got(i, s)
            z_forward(i, s).start()

    def z_sent(i, s):
        if s == 0:
            pl.when(t < lines - 1)(lambda: z_right(i, own_piece[i]).wait_send())
            pl.when(t > 0)(lambda: z_left(i, own_piece[i]).wait_send())
        else:
            pl.when(inner)(lambda: z_forward(i, s).wait_send())

    def gather_1(i, s):
        ref = piece(i, s, yx)
        return remote(ref, ref, pair(s_1, i, s - 1), dev_first)

    def gather_2(i, s, k):
        ref = piece(i, s, yx if k == 0 else yx_first)
        return remote(ref, ref, pair(s_2, i, s - 1, k), dev_second)

    def gather_3(i, s):
        ref = w_of[i].at[s, :, c]
        return remote(ref, ref, pair(s_3, i, s - 1), dev_core)

    def step_1(i, s):
        pl.when(outer)(lambda: z_got(i, s))
        gather_1(i, s).start()

    def step_2(i, s):
        gather_1(i, s).wait_recv()
        gather_2(i, s, 0).start()
        gather_2(i, s, 1).start()

    def step_3(i, s):
        gather_2(i, s, 0).wait_recv()
        gather_2(i, s, 1).wait_recv()
        gather_3(i, s).start()

    def step_4(i, s):
        gather_3(i, s).wait()
        gather_1(i, s).wait_send()
        gather_2(i, s, 0).wait_send()
        gather_2(i, s, 1).wait_send()

    def add_into(dst, src):
        dst[...] = (dst[...].astype(F32) + src[...].astype(F32)).astype(BF)

    send_k = [(1 - c) * (2 * k + 1 - x_bit) + c * (2 * (1 - y_bit) + k) for k in range(2)]
    keep_k = [(1 - c) * (2 * k + x_bit) + c * (2 * y_bit + k) for k in range(2)]
    k_mine = (1 - c) * y_bit + c * x_bit

    def reduce_core(i, s):
        return remote(w_of[i].at[s, :, 1 - c], r_core[i].at[s], pair(s_c, i, s), dev_core)

    def reduce_a(i, s, k):
        return remote(piece(i, s, send_k[k]), r_a[i].at[s, k], pair(s_a, i, s, k), dev_first)

    def reduce_b(i, s):
        return remote(piece(i, s, yx_second), r_b[i].at[s], pair(s_b, i, s), dev_second)

    def reduce_z(i, s):
        line = (0, by_line(1, 2, 3, 2), by_line(1, 0, 1, 2), by_line(1, 2, 1, 2))[s]
        place = (0, by_line(3, 3, 3, 4), by_line(0, 4, 4, 1), by_line(2, 0, 1, 2))[s]
        return remote(
            piece(i, s, yx), r_z[i].at[place], (s_zgs.at[i, s], s_zgr.at[i, place]), at(d, line)
        )

    def reduce_z_got(i, place):
        ref = r_z[i].at[place]
        remote(ref, ref, (s_zgs.at[i, 1], s_zgr.at[i, place]), dev_core).wait_recv()

    def fold_1(i, s):
        reduce_core(i, s).start()

    def fold_2(i, s):
        reduce_core(i, s).wait_recv()
        for k in range(2):
            add_into(piece(i, s, send_k[k]), r_core[i].at[s, send_k[k]])
            reduce_a(i, s, k).start()
        for k in range(2):
            add_into(piece(i, s, keep_k[k]), r_core[i].at[s, keep_k[k]])

    def fold_3(i, s):
        reduce_a(i, s, 0).wait_recv()
        reduce_a(i, s, 1).wait_recv()
        add_into(piece(i, s, yx_second), r_a[i].at[s, 1 - k_mine])
        reduce_b(i, s).start()
        add_into(piece(i, s, yx), r_a[i].at[s, k_mine])

    def fold_4(i, s):
        reduce_b(i, s).wait_recv()
        add_into(piece(i, s, yx), r_b[i].at[s])
        if s > 0:
            pl.when(outer)(lambda: reduce_z(i, s).start())

    def fold_5(i, s):
        @pl.when(inner)
        def _():
            reduce_z_got(i, s - 1)
            add_into(piece(i, s, yx), r_z[i].at[s - 1])
            reduce_z(i, s).start()

    def own_total(i, m):
        ref = piece(i, 0, yx)
        return ref if i == ATT else ref.at[m]

    def spread_1(i, m):
        dst = grads_out[i][m].at[yx, c]
        return remote(own_total(i, m), dst, pair(s_g1, i + m), dev_first)

    def spread_2(i, m, k):
        if k == 0:
            dst = grads_out[i][m].at[yx, c]
            return remote(own_total(i, m), dst, pair(s_g2, i + m, 0), dev_second)
        ref = grads_out[i][m].at[yx_first, c]
        return remote(ref, ref, pair(s_g2, i + m, 1), dev_second)

    def spread_3(i, m):
        ref = grads_out[i][m].at[:, c]
        return remote(ref, ref, pair(s_g3, i + m), dev_core)

    def keep_total(i, m):
        dst = grads_out[i][m].at[yx, c] if whole_plane else grads_out[i][m]
        return pltpu.make_async_copy(own_total(i, m), dst, s_loc.at[4 + i + m])

    def total(i):
        for side, there in ((3, t > 0), (4, t < lines - 1)):

            @pl.when(there)
            def _():
                reduce_z_got(i, side)
                add_into(piece(i, 0, yx), r_z[i].at[side])

        for m in range(1 + i):
            keep_total(i, m).start()
            if whole_plane:
                spread_1(i, m).start()

    def spread_step_2(i):
        if whole_plane:
            for m in range(1 + i):
                spread_2(i, m, 0).start()
            for m in range(1 + i):
                spread_1(i, m).wait_recv()
                spread_2(i, m, 1).start()

    def spread_step_3(i):
        for m in range(1 + i):
            keep_total(i, m).wait()
            if whole_plane:
                spread_2(i, m, 0).wait_recv()
                spread_2(i, m, 1).wait_recv()
                spread_3(i, m).start()

    ids_copy = remote(ids_in, ids.at[c], pair(s_ids), dev_core)
    ids_copy.start()
    own = [
        pltpu.make_async_copy(shard_qkv, w_att.at[0, pl.ds(0, 3)], s_loc.at[0]),
        pltpu.make_async_copy(shard_out, w_att.at[0, 3], s_loc.at[3]),
        pltpu.make_async_copy(shard_up, w_ffn.at[0, :, :, 0], s_loc.at[1]),
        pltpu.make_async_copy(shard_down, w_ffn.at[0, :, :, 1], s_loc.at[2]),
    ]
    for copy in own:
        copy.start()
    own_piece = (w_att.at[0, yx, c], w_ffn.at[0, yx, c])
    bias[0, 0:1, :] = bias_up[...][None]
    bias[0, 1:2, :part] = bias_qv[0:1]
    bias[0, 1:2, part : 2 * part] = bias_qv[1:2]
    bias[0, 1:2, 2 * part :] = jnp.zeros((1, width - 2 * part), F32)

    def bias_copy(s):
        line = source[s]
        slot = (0, by_line(2, 2, 1, 1), by_line(3, 1, 1, 3), by_line(3, 2, 2, 3))[s]
        return remote(bias.at[0], bias.at[slot], (s_bias.at[0, s], s_bias.at[1, slot]), at(d, line))

    def bias_got(s):
        remote(bias.at[s], bias.at[s], (s_bias.at[0, s], s_bias.at[1, s]), dev_core).wait_recv()

    for s in range(1, lines):
        bias_copy(s).start()
    ids[pl.ds(c, 1)] = ids_in[...][None]

    def see():
        remote(ids_in, ids.at[1 - c], pair(s_ids), dev_core).wait_recv()
        row = ids[t // 2, pl.ds(lax.rem(t, 2), 1), :].astype(F32)
        low, high = row[:, :half], row[:, half:]
        first_core = c == 0
        ids_own = jnp.where(first_core, low, high)
        ids_other = jnp.where(first_core, high, low)
        for place, ids_k in enumerate((ids_own, ids_other)):
            columns = jnp.broadcast_to(ids_k, (128, half)).T
            for j in range(0, half, 128):
                mask[place, :, j : j + 128] = jnp.where(columns == ids_own[:, j : j + 128], 0.0, -1e30)

    def att_weights(s):
        return w_att[s].reshape(width, width)

    def up_weights(s):
        return w_ffn[s, :, :, 0].reshape(width, width)

    def down_weights(s):
        return w_ffn[s, :, :, 1].reshape(width, width)

    def kv_copy(s):
        return remote(kv.at[s], kvs.at[s], pair(s_kv, s), dev_core)

    def project(s):
        qkv = dot(att_weights(s)[: 3 * part], n1[...], NT)
        bias_row = bias[s, 1:2, : 2 * part]
        bias_col = jnp.broadcast_to(bias_row, (128, 2 * part)).T[:, :1]
        qt[s] = (qkv[:part] + bias_col[:part]).astype(BF)
        kv[s, 0] = qkv[part : 2 * part].astype(BF)
        kv[s, 1] = (qkv[2 * part :] + bias_col[part:]).astype(BF)
        kv_copy(s).start()

    def kvg_copy(s):
        return remote(kvs.at[s], kvg.at[s], pair(s_kvg, s), dev_core)

    def finish(s):
        kvg_copy(s).wait_recv()
        dq = qt[s]
        dkv = (kv[s].astype(F32) + kvg[s].astype(F32)).astype(BF).reshape(2 * part, half)
        ones = jnp.ones((8, half), BF)
        sums[s, 1:2, :part] = dot(ones, dq, NT)[:1]
        sums[s, 1:2, part : 2 * part] = dot(ones, dkv[part:], NT)[:1]
        sums[s, 1:2, 2 * part :] = jnp.zeros((1, width - 2 * part), F32)
        stacked = jnp.concatenate([dq, dkv], axis=0)
        acc[...] += dot(stacked, att_weights(s)[: 3 * part], TN)
        w_att[s, 0:3] = dot(stacked, n1[...], NN).astype(BF).reshape(3, 2, 96, width)
        fold_1(ATT, s)

    def sums_copy(s):
        return remote(
            sums.at[s],
            sums_z.at[t],
            (s_sz.at[0, s], s_sz.at[1, t]),
            at(d, source[s]),
        )

    def sums_got(s):
        ref = sums_z.at[source[s]]
        remote(ref, ref, (s_sz.at[0, s], s_sz.at[1, source[s]]), dev_core).wait_recv()

    dev_x = at(base + 2 * yx_x + c, t)
    dev_y = at(base + 2 * yx_y + c, t)

    def flip(k):
        return remote(
            sums_p.at[2 * k], sums_p.at[2 * k + 1], pair(s_sp, k), (dev_core, dev_x, dev_y)[k]
        )

    def sums_start():
        for s in range(1, lines):
            sums_copy(s).start()
        sums_z[pl.ds(t, 1)] = sums[0:1]

    def sums_line():
        for s in range(1, lines):
            sums_got(s)
        sums_p[0] = (sums_z[0] + sums_z[1]) + (sums_z[2] + sums_z[3])
        flip(0).start()

    def sums_plane(k):
        flip(k - 1).wait()
        sums_p[2 * k] = sums_p[2 * k - 2] + sums_p[2 * k - 1]
        flip(k).start()

    def sums_end():
        flip(2).wait()
        small_out[...] = sums_p[4] + sums_p[5]

    steps = {
        Z_OWN: z_own,
        Z_PASS: z_pass,
        STEP_1: step_1,
        STEP_2: step_2,
        STEP_3: step_3,
        FOLD_2: fold_2,
        FOLD_3: fold_3,
        FOLD_4: fold_4,
        FOLD_5: fold_5,
        TOTAL: total,
        SPREAD_2: spread_step_2,
        SPREAD_3: spread_step_3,
        FINISH: finish,
        SEE: see,
        SUMS: sums_start,
        SUMS_Z: sums_line,
        SUMS_P: sums_plane,
        SUMS_END: sums_end,
        MOVE: lambda name, *which: to_owner(*rows[name], *which),
    }
    rows = {
        X: (tokens, xb, s_x),
        G: (cotangent, gb, s_g),
        BO: (bo, block_home, s_bo),
        IG: (ig, input_home, s_ig),
    }

    def run(*where):
        for name, *which in PLAN.get(where, ()):
            steps[name](*which)

    def point(loop, j, where):
        for k in range(lines):
            if (loop, k, where) in PLAN:
                pl.when(j == k)(functools.partial(run, loop, k, where))

    run(START)
    to_owner_wait(tokens, xb, s_x)
    run(X_HERE)
    normed, _ = norm_parts(xb[...].reshape(half, width).astype(F32))
    n1[...] = (normed * gain_first + shift_first).astype(BF)
    for s in range(1, lines):
        bias_got(s)
    project(0)
    run(FIRST)

    def attend(s, carry):
        @pl.when(s < lines - 1)
        def _():
            step_4(ATT, s + 1)
            project(s + 1)

        kv_copy(s).wait_recv()
        for h in range(part // HEAD):
            rows = slice(h * HEAD, (h + 1) * HEAD)
            q = qt[s, rows, :]
            s0 = dot(kv[s, 0, rows, :].T, q, NN) * FACTOR + mask[0]
            s1 = dot(kvs[s, 0, rows, :].T, q, NN) * FACTOR + mask[1]
            top = jnp.maximum(
                jnp.max(s0, axis=0, keepdims=True), jnp.max(s1, axis=0, keepdims=True)
            )
            p0 = jnp.exp2(s0 - top)
            p1 = jnp.exp2(s1 - top)
            weight = column_sum(p0) + column_sum(p1)
            out = dot(kv[s, 1, rows, :], p0.astype(BF), NN)
            out = out + dot(kvs[s, 1, rows, :], p1.astype(BF), NN)
            ct[s, rows, :] = (out / weight).astype(BF)
            lse[s, h : h + 1, :] = top + jnp.log2(weight)
            point(ATTEND, s, h)
        return carry

    lax.fori_loop(0, lines, attend, 0)

    mid = xb[...].reshape(half, width).astype(F32) + bias_out
    for s in range(lines):
        mid = mid + dot(ct[s], att_weights(s)[3 * part :], TN)
    middle[...] = mid
    normed, _ = norm_parts(mid)
    low_normed = (normed * gain_second + shift_second).astype(BF)
    n2[...] = low_normed
    n2t[...] = low_normed.T
    acc[...] = jnp.zeros_like(acc)
    acc2[...] = jnp.zeros_like(acc2)
    run(OUT)
    to_owner_wait(cotangent, gb, s_g)

    def feed(s, carry):
        @pl.when(s > 0)
        def _():
            step_4(FFN, s)

        for k in range(lines):
            pl.when(s == k)(functools.partial(z_sent, FFN, k))
        point(FEED, s, 0)
        grad = gb[...].reshape(half, width)
        pre = dot(n2[...], up_weights(s), NN) + bias[s, 0:1, :]
        phi = 0.5 * (1.0 + lax.erf(pre * 0.7071067811865476))
        active = (pre * phi).astype(BF)
        slope = phi + pre * jnp.exp(-0.5 * pre * pre) * 0.3989422804014327
        acc[...] += dot(active, down_weights(s), NN)
        point(FEED, s, 1)
        pre_grad = (dot(grad, down_weights(s), NT) * slope).astype(BF)
        sums[s, 0:1, :] = column_sum(pre_grad.astype(F32))
        point(FEED, s, 2)
        acc2[...] += dot(pre_grad, up_weights(s), NT)
        point(FEED, s, 3)
        w_ffn[s, :, :, 1] = dot(active, grad, TN).astype(BF).reshape(4, 2, 96, width)
        point(FEED, s, 4)
        w_ffn[s, :, :, 0] = dot(n2t[...], pre_grad, NN).astype(BF).reshape(4, 2, 96, width)
        fold_1(FFN, s)
        point(FEED, s, 5)
        return carry

    lax.fori_loop(0, lines, feed, 0)

    mid = middle[...]
    bo[...] = (mid + acc[...] + bias_down).astype(BF).reshape(2, 256, width)
    run(BLOCK)
    normed, rate = norm_parts(mid)
    grad = gb[...].reshape(half, width).astype(F32)
    back = acc2[...]
    middle_grad = grad + norm_back(normed, rate, back, gain_second)
    vec_out = column_sum(middle_grad)
    vec_gain = column_sum(back * normed)
    vec_shift = column_sum(back)
    vec_down = column_sum(grad)
    for s in range(lines):
        sums[s, 4:5, :] = vec_out
        sums[s, 5:6, :] = vec_gain
        sums[s, 6:7, :] = vec_shift
        sums[s, 7:8, :] = vec_down
    acc2[...] = middle_grad
    dmr[...] = middle_grad.astype(BF)
    acc[...] = jnp.zeros_like(acc)
    for s in range(lines):
        z_sent(ATT, s)
    run(NORM)

    def attend_back(j, carry):
        s = by_line_of(j, *ORDER)
        dct = dot(w_att[s, 3].reshape(part, width), dmr[...], NT).astype(BF)
        w_att[s, 3] = dot(ct[s], dmr[...], NN).astype(BF).reshape(2, 96, width)
        kv_copy(s).wait_send()
        point(BACK, j, 0)
        for h in range(part // HEAD):
            rows = slice(h * HEAD, (h + 1) * HEAD)
            g = dct[rows]
            q = qt[s, rows, :]
            along = column_sum(g.astype(F32) * ct[s, rows, :].astype(F32))
            total_log = lse[s, h : h + 1, :]
            dq = jnp.zeros((HEAD, half), F32)
            for place, ref in enumerate((kv, kvs)):
                k = ref[s, 0, rows, :]
                v = ref[s, 1, rows, :]
                p = jnp.exp2(dot(k.T, q, NN) * FACTOR + mask[place] - total_log)
                ds = (p * (dot(v.T, g, NN) - along)).astype(BF)
                ref[s, 0, rows, :] = (dot(q, ds, NT) * HEAD**-0.5).astype(BF)
                ref[s, 1, rows, :] = dot(g, p.astype(BF), NT).astype(BF)
                dq = dq + dot(k, ds, NN)
            qt[s, rows, :] = (dq * HEAD**-0.5).astype(BF)
            if h == part // HEAD - 1:
                kvg_copy(s).start()
            point(BACK, j, h + 1)
        return carry

    lax.fori_loop(0, lines, attend_back, 0)
    run(TAIL_0)

    normed, rate = norm_parts(xb[...].reshape(half, width).astype(F32))
    back = acc[...]
    vec_gain = column_sum(back * normed)
    vec_shift = column_sum(back)
    for s in range(lines):
        sums[s, 2:3, :] = vec_gain
        sums[s, 3:4, :] = vec_shift

    run(TAIL_1)
    ig[...] = (
        (acc2[...] + norm_back(normed, rate, back, gain_first))
        .astype(BF)
        .reshape(2, 256, width)
    )
    run(TAIL_2)
    run(TAIL_3)

    ids_copy.wait_send()
    for s in range(1, lines):
        bias_copy(s).wait_send()
        sums_copy(s).wait_send()
    to_owner_sent(tokens, s_x)
    to_owner_sent(cotangent, s_g)
    to_owner_wait(bo, block_home, s_bo)
    to_owner_sent(bo, s_bo)
    for s in range(lines):
        kvg_copy(s).wait_send()
    for i in (ATT, FFN):
        for s in range(lines):
            reduce_core(i, s).wait_send()
            reduce_a(i, s, 0).wait_send()
            reduce_a(i, s, 1).wait_send()
            reduce_b(i, s).wait_send()
            if s > 0:
                reduce_z(i, s).wait_send()
        for m in range(1 + i if whole_plane else 0):
            spread_1(i, m).wait_send()
            spread_2(i, m, 0).wait_send()
            spread_2(i, m, 1).wait_send()
            spread_3(i, m).wait()
    to_owner_wait(ig, input_home, s_ig)
    to_owner_sent(ig, s_ig)


def layer(lines, whole_plane, operands):
    def dma(*shape):
        return pltpu.SemaphoreType.DMA((2,) + shape)

    def vmem(*shape, dtype=BF):
        return pltpu.VMEM(shape, dtype)

    n = lines
    anywhere = pl.BlockSpec(memory_space=pl.ANY)
    inside = pl.BlockSpec(memory_space=pltpu.VMEM)
    att = (96, 768)
    ffn = (2, 96, 768)
    plane = (4, 2) if whole_plane else ()
    blocks = jax.ShapeDtypeStruct((2, 256, 768), BF)
    return pl.pallas_call(
        functools.partial(layer_kernel, lines, whole_plane),
        in_specs=[anywhere, anywhere, inside] + [anywhere] * 4 + [inside] * 8,
        out_specs=[anywhere] * 5 + [inside],
        out_shape=[
            blocks,
            blocks,
            jax.ShapeDtypeStruct(plane + att, BF),
            jax.ShapeDtypeStruct(plane + att, BF),
            jax.ShapeDtypeStruct(plane + att, BF),
            jax.ShapeDtypeStruct((8, 768), F32),
        ],
        scratch_shapes=[
            vmem(n, 4, 2, *att),
            vmem(n, 4, 2, *ffn),
            vmem(n, 4, *att),
            vmem(n, 4, *ffn),
            vmem(n, 2, *att),
            vmem(n, 2, *ffn),
            vmem(n, *att),
            vmem(n, *ffn),
            vmem(5, *att),
            vmem(5, *ffn),
            vmem(2, 256, 768),
            vmem(2, 256, 768),
            vmem(2, 2, 1024, dtype=jnp.int32),
            vmem(n, 8, 768, dtype=F32),
            vmem(2, 512, 512, dtype=F32),
            vmem(512, 768),
            vmem(512, 768),
            vmem(768, 512),
            vmem(512, 768, dtype=F32),
            vmem(512, 768, dtype=F32),
            vmem(512, 768, dtype=F32),
            vmem(512, 768),
            vmem(n, 192, 512),
            vmem(n, 2, 192, 512),
            vmem(n, 2, 192, 512),
            vmem(n, 2, 192, 512),
            vmem(n, 192, 512),
            vmem(n, 8, 512, dtype=F32),
            vmem(2, 256, 768),
            vmem(2, 256, 768),
            vmem(n, 8, 768, dtype=F32),
            vmem(n, 8, 768, dtype=F32),
            vmem(6, 8, 768, dtype=F32),
            pltpu.SemaphoreType.DMA((7,)),
            dma(),
            dma(n),
            dma(2, 2),
            dma(2, 2),
            dma(2, 2),
            dma(2, 2),
            dma(n),
            dma(n),
            pltpu.SemaphoreType.DMA((2, 5)),
            pltpu.SemaphoreType.DMA((2, n)),
            dma(2, n - 1),
            dma(2, n - 1, 2),
            dma(2, n - 1),
            dma(2, n),
            dma(2, n, 2),
            dma(2, n),
            pltpu.SemaphoreType.DMA((2, n)),
            pltpu.SemaphoreType.DMA((2, 5)),
            dma(3),
            dma(3, 2),
            dma(3),
            dma(n),
            dma(3),
        ],
        compiler_params=pltpu.CompilerParams(
            collective_id=0, has_side_effects=True, vmem_limit_bytes=62 * 2**20
        ),
        name="layer",
    )(*operands)


def results_kernel(
    block_in, input_in, att_in, up_in, down_in, small_in,
    block_out, input_out, qkv_out, out_out, up_out, down_out, bias_out, *rest
):
    sums_out, (low_in, low_att, low_up, low_down) = rest[:7], rest[7:11]
    wide_in, wide_att, wide_up, wide_down, low_block, s_in, s_out, s_block = rest[11:]
    part = bias_out.shape[1]
    third = 3 * part
    block = pltpu.make_async_copy(block_in, low_block, s_block)
    jobs = [(up_in, low_up, wide_up, up_out, 0, 0, 2 * part)]
    jobs += [(up_in, low_up, wide_up, up_out, 2 * part, 2 * part, 2 * part)]
    jobs += [(down_in, low_down, wide_down, down_out, k, k, 2 * part) for k in (0, 2 * part)]
    jobs += [(att_in, low_att, wide_att, qkv_out, 0, 0, third)]
    jobs += [(att_in, low_att, wide_att, out_out, third, 0, part)]
    jobs += [(input_in, low_in, wide_in, input_out, k, k, 256) for k in (0, 256)]

    def fetch(k):
        source, low, _, _, at, _, size = jobs[k]
        rows = pl.ds(at, size)
        return pltpu.make_async_copy(source.at[rows], low.at[rows], s_in.at[k])

    def store(k):
        _, _, wide, result, at, to, size = jobs[k]
        return pltpu.make_async_copy(wide.at[pl.ds(at, size)], result.at[pl.ds(to, size)], s_out.at[k])

    for k in range(len(jobs)):
        fetch(k).start()
    block.start()
    bias_out[0:1] = small_in[1:2, :part]
    bias_out[1:2] = small_in[1:2, part : 2 * part]
    for ref, row in zip(sums_out, (0, 2, 3, 4, 5, 6, 7)):
        ref[...] = small_in[row]
    for k, (_, low, wide, _, at, _, size) in enumerate(jobs):
        fetch(k).wait()
        wide[pl.ds(at, size)] = low[pl.ds(at, size)].astype(F32)
        store(k).start()
    block.wait()
    block = pltpu.make_async_copy(low_block, block_out, s_block)
    block.start()
    for k in range(len(jobs)):
        store(k).wait()
    block.wait()


def results(block, inputs, att, up, down, small):
    width = att.shape[0]
    part = width // 4
    tokens = inputs.shape[0] * inputs.shape[1]
    anywhere = pl.BlockSpec(memory_space=pl.ANY)
    inside = pl.BlockSpec(memory_space=pltpu.VMEM)
    shapes = ((tokens, width), (width, width), (width, width), (width, width))
    block, inputs, *results = pl.pallas_call(
        results_kernel,
        in_specs=[anywhere] * 5 + [inside],
        out_specs=[anywhere] * 6 + [inside] * 8,
        out_shape=[
            jax.ShapeDtypeStruct(block.shape, BF),
            jax.ShapeDtypeStruct((tokens, width), F32),
            jax.ShapeDtypeStruct((3 * part, width), F32),
            jax.ShapeDtypeStruct((part, width), F32),
            jax.ShapeDtypeStruct((width, width), F32),
            jax.ShapeDtypeStruct((width, width), F32),
            jax.ShapeDtypeStruct((2, part), F32),
        ]
        + [jax.ShapeDtypeStruct((width,), F32)] * 7,
        scratch_shapes=[pltpu.VMEM(shape, BF) for shape in shapes]
        + [pltpu.VMEM(shape, F32) for shape in shapes]
        + [pltpu.VMEM(block.shape, BF)]
        + [pltpu.SemaphoreType.DMA((8,)), pltpu.SemaphoreType.DMA((8,)), pltpu.SemaphoreType.DMA],
        compiler_params=pltpu.CompilerParams(vmem_limit_bytes=62 * 2**20),
        name="results",
    )(block, inputs.reshape(tokens, width), att, up, down, small)
    return (block, inputs.reshape(block.shape), *results)


def body(
    dp,
    lines,
    tokens,
    segment_ids,
    gain_first,
    shift_first,
    weight_qkv,
    bias_qv,
    weight_out,
    bias_out,
    gain_second,
    shift_second,
    weight_up,
    bias_up,
    weight_down,
    bias_down,
    cotangent,
):
    width = tokens.shape[2]
    part = weight_qkv.shape[2]
    shard = (4, 2, width // PLANE, width)
    whole_plane = dp == PLANE
    block_out, input_grad, *grads, small = layer(
        lines,
        whole_plane,
        (
            tokens,
            cotangent,
            segment_ids,
            weight_qkv.reshape(width, 3 * part).T.reshape(3, 2, width // PLANE, width),
            weight_out.reshape(2, width // PLANE, width),
            weight_up.reshape(shard),
            weight_down.reshape(shard),
            bias_up,
            bias_qv,
            gain_first,
            shift_first,
            bias_out,
            gain_second,
            shift_second,
            bias_down,
        ),
    )
    if not whole_plane:
        apart = [[i + PLANE * g for g in range(dp // PLANE)] for i in range(PLANE)]
        planes = [[i + PLANE * g for i in range(PLANE)] for g in range(dp // PLANE)]
        sums = tuple(grad.astype(F32) for grad in grads)
        *grads, small = lax.psum(sums + (small,), "dp", axis_index_groups=apart)
        grads = [lax.all_gather(g.astype(BF), "dp", axis_index_groups=planes) for g in grads]
    att_grad, up_grad, down_grad = [grad.reshape(width, width) for grad in grads]
    block_out, input_grad, qkv_grad, out_grad, up_grad, down_grad, bias_grad, *sums = results(
        block_out, input_grad, att_grad, up_grad, down_grad, small
    )
    up_bias, gain_one, shift_one, out_bias, gain_two, shift_two, down_bias = sums
    return (
        block_out,
        input_grad,
        gain_one,
        shift_one,
        qkv_grad.T.reshape(width, 3, part),
        bias_grad,
        out_grad,
        out_bias,
        gain_two,
        shift_two,
        up_grad,
        up_bias,
        down_grad,
        down_bias,
    )


def solution(mesh):
    in_specs = (
        P("dp", "tensor", None),
        P("dp", None),
        P(),
        P(),
        P(None, None, "tensor"),
        P(None, "tensor"),
        P("tensor", None),
        P(),
        P(),
        P(),
        P(None, "tensor"),
        P("tensor"),
        P("tensor", None),
        P(),
        P("dp", "tensor", None),
    )
    out_specs = (
        P("dp", "tensor", None),
        P("dp", "tensor", None),
        P(),
        P(),
        P(None, None, "tensor"),
        P(None, "tensor"),
        P("tensor", None),
        P(),
        P(),
        P(),
        P(None, "tensor"),
        P("tensor"),
        P("tensor", None),
        P(),
    )
    whole = functools.partial(body, mesh.shape["dp"], mesh.shape["tensor"])
    return jax.shard_map(whole, mesh=mesh, in_specs=in_specs, out_specs=out_specs, check_vma=False)
```

time: 224 us -> 170 us (0.76)
  Pallas kernels: 205 us -> 169 us
  local copies, waits for them, and re-layouts: 10.4 us -> 0 us
  other arithmetic: 7.17 us -> 0 us
    pallas_call x1, Pallas kernels: 205 us -> 163 us  [layer(): pl.pallas_call(functools.partial(layer_kernel, lines, whole_plane), in_sp...]
    slice x5 -> x0, local copies, waits for them, and re-layouts: 7.33 us -> none  [the longest x1 2.69 us: body(): grads[2]]
    pallas_call x0 -> x1, Pallas kernels: none -> 6.26 us  [results(): pl.pallas_call(results_kernel, in_specs=[anywhere] * 5 + [inside], out_sp...]
    convert_element_type x2 -> x0, other arithmetic: 4.1 us -> none  [the longest x1 2.85 us: body(): grads = grads.reshape(3, width, width).astype(F32)]
    concatenate x2 -> x0, other arithmetic: 3.07 us -> none  [the longest x1 2.39 us: body(): jnp.concatenate([weight_qkv.reshape(width, 3 * part).T, weight_out], axis=0)]
where the time goes in v3:
time: 170 us
  Pallas kernels  169 us (99%)
    pallas_call x1, Pallas kernels, layer(): pl.pallas_call(functools.partial(layer_kernel, lines, whole_plane), in_sp...  163 us
    pallas_call x1, Pallas kernels, results(): pl.pallas_call(results_kernel, in_specs=[anywhere] * 5 + [inside], out_sp...  6.26 us

profile of v3, /device:TPU:0, one launch (start us, length us, event | category | flops | bytes accessed | tf_op | source)
XLA Modules:
  0.0 169.7 jit_solution(8741593675507410307)
XLA Ops:
  0.7 162.6 %layer.1 = (bf16[2,256,768]{2,1,0:T(8,128)(2,1)}, bf16[2,256,768]{2,1,0:T(8,128)(2,1)}, bf16[4,2,96,768]{3,2,1,0:T(8,128)(2,1)}, bf16[4,2,96,768]{3,2,1,0:T(8,12...) custom-call(bf16[2,256,768]{2,1,0:T(8,128)(2,1)} %tokens.1, bf16[2,256,768]{2,1,0:T(8,128)(2,1)} %cotangent.1, ...), custom_call_target="tpu_custom_call" | custom-call | tf_op jit(solution)/shard_map/layer/pallas_call | solution.py:915
  163.3 6.3 %results.1 = (bf16[2,256,768]{2,1,0:T(8,128)(2,1)}, f32[512,768]{1,0:T(8,128)}, f32[576,768]{1,0:T(8,128)}, f32[192,768]{1,0:T(8,128)}, f32[768,768]{1,0:T(8,128...) custom-call(bf16[2,256,768]{2,1,0:T(8,128)(2,1)} %get-tuple-element., ...), custom_call_target="tpu_custom_call" | custom-call | tf_op jit(solution)/shard_map/results/pallas_call | solution.py:1044

commit v4 on v3

--- a/solution.py
+++ b/solution.py
@@ -27,148 +27,146 @@
 PLAN = {
     (START,): (
         (Z_OWN, ATT),
+        (MOVE, X, 0, 0),
+        (MOVE, X, 1, 1),
+        (Z_PASS, ATT, 1),
+        (Z_PASS, ATT, 2),
+        (STEP_1, ATT, 1),
         (Z_OWN, FFN),
-        (Z_PASS, ATT, 1),
-        (MOVE, X, 0, 0),
+        (STEP_1, ATT, 2),
+        (STEP_2, ATT, 1),
+        (Z_PASS, ATT, 3),
+        (MOVE, X, 0, 1),
+        (MOVE, X, 1, 0),
+        (STEP_1, ATT, 3),
+        (SEE,),
         (Z_PASS, FFN, 1),
-        (STEP_1, ATT, 1),
-        (MOVE, X, 1, 1),
-        (Z_PASS, ATT, 2),
         (STEP_1, FFN, 1),
-        (MOVE, X, 0, 1),
-        (STEP_2, ATT, 1),
-        (STEP_1, ATT, 2),
-        (SEE,),
+        (STEP_2, ATT, 2),
+    ),
+    (X_HERE,): (
+        (MOVE, G, 0, 0),
         (Z_PASS, FFN, 2),
-        (MOVE, X, 1, 0),
-        (STEP_2, ATT, 2),
+        (STEP_3, ATT, 1),
+        (STEP_2, ATT, 3),
+    ),
+    (FIRST,): (
+        (STEP_3, ATT, 2),
+        (STEP_1, FFN, 2),
+    ),
+    (ATTEND, 0, 0): (
         (STEP_2, FFN, 1),
-        (Z_PASS, ATT, 3),
-    ),
-    (X_HERE,): (
-        (MOVE, G, 0, 1),
-        (STEP_3, ATT, 1),
-        (STEP_1, ATT, 3),
-    ),
-    (FIRST,): (
-        (STEP_1, FFN, 2),
-    ),
-    (ATTEND, 0, 0): (
-        (STEP_3, ATT, 2),
-    ),
-    (ATTEND, 0, 1): (
-        (STEP_2, ATT, 3),
-    ),
-    (ATTEND, 0, 2): (
+        (MOVE, G, 1, 0),
+    ),
+    (ATTEND, 1, 0): (
         (Z_PASS, FFN, 3),
-        (MOVE, G, 0, 0),
-        (MOVE, G, 1, 0),
-    ),
-    (ATTEND, 1, 1): (
-        (STEP_2, FFN, 2),
         (MOVE, G, 1, 1),
     ),
     (ATTEND, 1, 2): (
         (STEP_3, ATT, 3),
-    ),
-    (ATTEND, 2, 0): (
+        (STEP_2, FFN, 2),
+        (MOVE, G, 0, 1),
+    ),
+    (ATTEND, 2, 2): (
         (STEP_3, FFN, 1),
     ),
-    (ATTEND, 3, 0): (
+    (ATTEND, 3, 2): (
         (STEP_1, FFN, 3),
     ),
-    (OUT,): (
+    (FEED, 0, 3): (
         (STEP_3, FFN, 2),
-    ),
-    (FEED, 0, 2): (
         (STEP_2, FFN, 3),
     ),
-    (FEED, 1, 5): (
+    (FEED, 2, 1): (
         (FOLD_2, FFN, 0),
         (STEP_3, FFN, 3),
     ),
-    (FEED, 2, 5): (
+    (FEED, 2, 3): (
         (FOLD_2, FFN, 1),
     ),
     (BLOCK,): (
+        (MOVE, BO, 1, 1),
+    ),
+    (BACK, 0, 1): (
+        (FOLD_2, FFN, 3),
+    ),
+    (BACK, 0, 3): (
+        (MOVE, BO, 1, 0),
+    ),
+    (BACK, 1, 0): (
         (MOVE, BO, 0, 0),
-        (MOVE, BO, 1, 1),
-    ),
-    (NORM,): (
-        (MOVE, BO, 1, 0),
-    ),
-    (BACK, 0, 0): (
         (FOLD_2, FFN, 2),
     ),
-    (BACK, 1, 0): (
-        (FOLD_2, FFN, 3),
+    (BACK, 1, 1): (
         (FINISH, 3),
+        (FOLD_3, FFN, 3),
     ),
     (BACK, 1, 2): (
         (FOLD_2, ATT, 3),
     ),
     (BACK, 1, 3): (
         (MOVE, BO, 0, 1),
-        (FOLD_3, FFN, 3),
-        (FOLD_3, FFN, 2),
         (FINISH, 2),
     ),
     (BACK, 2, 0): (
         (FOLD_4, FFN, 3),
+    ),
+    (BACK, 2, 1): (
+        (FOLD_3, FFN, 2),
+    ),
+    (BACK, 3, 0): (
         (FOLD_3, ATT, 3),
-    ),
-    (BACK, 2, 3): (
+        (FOLD_3, FFN, 1),
+    ),
+    (BACK, 3, 1): (
+        (FOLD_4, FFN, 2),
+        (FOLD_5, FFN, 3),
         (FOLD_2, ATT, 2),
+    ),
+    (BACK, 3, 2): (
+        (FINISH, 1),
+        (FOLD_3, FFN, 0),
+    ),
+    (BACK, 3, 3): (
         (FOLD_4, ATT, 3),
-        (FOLD_3, FFN, 1),
-    ),
-    (BACK, 3, 0): (
-        (FOLD_5, FFN, 3),
-        (FOLD_4, FFN, 2),
-        (FOLD_3, FFN, 0),
-    ),
-    (BACK, 3, 1): (
-        (FINISH, 1),
+        (FOLD_4, FFN, 1),
+        (FOLD_2, ATT, 1),
+        (FOLD_5, FFN, 2),
+        (FOLD_5, FFN, 1),
+    ),
+    (TAIL_0,): (
+        (FINISH, 0),
+        (FOLD_3, ATT, 2),
+    ),
+    (TAIL_1,): (
+        (FOLD_2, ATT, 0),
         (FOLD_5, ATT, 3),
-    ),
-    (BACK, 3, 2): (
-        (FOLD_3, ATT, 2),
-    ),
-    (BACK, 3, 3): (
-        (FOLD_4, FFN, 1),
-        (FOLD_5, FFN, 1),
-        (FOLD_2, ATT, 1),
-    ),
-    (TAIL_0,): (
-        (FOLD_5, FFN, 2),
-        (FINISH, 0),
+        (FOLD_3, ATT, 1),
+    ),
+    (TAIL_2,): (
         (FOLD_4, FFN, 0),
-    ),
-    (TAIL_2,): (
+        (FOLD_4, ATT, 2),
         (SUMS,),
-        (FOLD_4, ATT, 2),
-        (MOVE, IG, 1, 1),
-        (FOLD_3, ATT, 1),
-        (FOLD_2, ATT, 0),
+        (MOVE, IG, 1, 0),
         (TOTAL, FFN),
-    ),
-    (TAIL_3,): (
+        (FOLD_3, ATT, 0),
         (FOLD_4, ATT, 1),
         (FOLD_5, ATT, 2),
+        (SUMS_Z,),
         (MOVE, IG, 0, 1),
+    ),
+    (TAIL_3,): (
+        (FOLD_4, ATT, 0),
         (FOLD_5, ATT, 1),
-        (SUMS_Z,),
+        (SUMS_P, 1),
+        (SPREAD_2, FFN),
+        (MOVE, IG, 1, 1),
+        (TOTAL, ATT),
         (MOVE, IG, 0, 0),
-        (FOLD_3, ATT, 0),
-        (MOVE, IG, 1, 0),
-        (SPREAD_2, FFN),
-        (SUMS_P, 1),
-        (FOLD_4, ATT, 0),
-        (TOTAL, ATT),
         (SPREAD_2, ATT),
+        (SUMS_P, 2),
         (SPREAD_3, FFN),
         (SPREAD_3, ATT),
-        (SUMS_P, 2),
         (SUMS_END,),
     ),
 }
@@ -459,7 +457,7 @@
         gather_2(i, s, 1).wait_send()
 
     def add_into(dst, src):
-        dst[...] = (dst[...].astype(F32) + src[...].astype(F32)).astype(BF)
+        dst[...] = dst[...] + src[...]
 
     send_k = [(1 - c) * (2 * k + 1 - x_bit) + c * (2 * (1 - y_bit) + k) for k in range(2)]
     keep_k = [(1 - c) * (2 * k + x_bit) + c * (2 * y_bit + k) for k in range(2)]

time: 170 us -> 167 us (0.982)
  Pallas kernels: 169 us -> 165 us
    pallas_call x1, Pallas kernels: 163 us -> 159 us  [layer(): pl.pallas_call(functools.partial(layer_kernel, lines, whole_plane), in_sp...]
where the time goes in v4:
time: 167 us; the launch traced here: 166 us
  Pallas kernels  165 us (99%)
    pallas_call x1, Pallas kernels, layer(): pl.pallas_call(functools.partial(layer_kernel, lines, whole_plane), in_sp...  159 us
    pallas_call x1, Pallas kernels, results(): pl.pallas_call(results_kernel, in_specs=[anywhere] * 5 + [inside], out_sp...  6.26 us

profile of v4, /device:TPU:0, one launch (start us, length us, event | category | flops | bytes accessed | tf_op | source)
XLA Modules:
  0.0 166.0 jit_solution(16380776660659720814)
XLA Ops:
  0.7 158.9 %layer.1 = (bf16[2,256,768]{2,1,0:T(8,128)(2,1)}, bf16[2,256,768]{2,1,0:T(8,128)(2,1)}, bf16[4,2,96,768]{3,2,1,0:T(8,128)(2,1)}, bf16[4,2,96,768]{3,2,1,0:T(8,12...) custom-call(bf16[2,256,768]{2,1,0:T(8,128)(2,1)} %tokens.1, bf16[2,256,768]{2,1,0:T(8,128)(2,1)} %cotangent.1, ...), custom_call_target="tpu_custom_call" | custom-call | tf_op jit(solution)/shard_map/layer/pallas_call | solution.py:913
  159.6 6.3 %results.1 = (bf16[2,256,768]{2,1,0:T(8,128)(2,1)}, f32[512,768]{1,0:T(8,128)}, f32[576,768]{1,0:T(8,128)}, f32[192,768]{1,0:T(8,128)}, f32[768,768]{1,0:T(8,128...) custom-call(bf16[2,256,768]{2,1,0:T(8,128)(2,1)} %get-tuple-element., ...), custom_call_target="tpu_custom_call" | custom-call | tf_op jit(solution)/shard_map/results/pallas_call | solution.py:1042

commit v5 on v4

--- a/solution.py
+++ b/solution.py
@@ -765,7 +765,7 @@
     low_normed = (normed * gain_second + shift_second).astype(BF)
     n2[...] = low_normed
     n2t[...] = low_normed.T
-    acc[...] = jnp.zeros_like(acc)
+    acc[...] = mid + bias_down
     acc2[...] = jnp.zeros_like(acc2)
     run(OUT)
     to_owner_wait(cotangent, gb, s_g)
@@ -786,7 +786,7 @@
         acc[...] += dot(active, down_weights(s), NN)
         point(FEED, s, 1)
         pre_grad = (dot(grad, down_weights(s), NT) * slope).astype(BF)
-        sums[s, 0:1, :] = column_sum(pre_grad.astype(F32))
+        sums[s, 0:1, :] = dot(jnp.ones((8, half), BF), pre_grad, NN)[:1]
         point(FEED, s, 2)
         acc2[...] += dot(pre_grad, up_weights(s), NT)
         point(FEED, s, 3)
@@ -800,7 +800,7 @@
     lax.fori_loop(0, lines, feed, 0)
 
     mid = middle[...]
-    bo[...] = (mid + acc[...] + bias_down).astype(BF).reshape(2, 256, width)
+    bo[...] = acc[...].astype(BF).reshape(2, 256, width)
     run(BLOCK)
     normed, rate = norm_parts(mid)
     grad = gb[...].reshape(half, width).astype(F32)

time: 167 us -> 169 us (1.012)
  no operation moved by 1% of the time
where the time goes in v5:
time: 169 us; the launch traced here: 167 us
  Pallas kernels  166 us (98%)
    pallas_call x1, Pallas kernels, layer(): pl.pallas_call(functools.partial(layer_kernel, lines, whole_plane), in_sp...  160 us
    pallas_call x1, Pallas kernels, results(): pl.pallas_call(results_kernel, in_specs=[anywhere] * 5 + [inside], out_sp...  6.26 us

profile of v5, /device:TPU:0, one launch (start us, length us, event | category | flops | bytes accessed | tf_op | source)
XLA Modules:
  0.0 167.1 jit_solution(6040821112284442890)
XLA Ops:
  0.7 160.1 %layer.1 = (bf16[2,256,768]{2,1,0:T(8,128)(2,1)}, bf16[2,256,768]{2,1,0:T(8,128)(2,1)}, bf16[4,2,96,768]{3,2,1,0:T(8,128)(2,1)}, bf16[4,2,96,768]{3,2,1,0:T(8,12...) custom-call(bf16[2,256,768]{2,1,0:T(8,128)(2,1)} %tokens.1, bf16[2,256,768]{2,1,0:T(8,128)(2,1)} %cotangent.1, ...), custom_call_target="tpu_custom_call" | custom-call | tf_op jit(solution)/shard_map/layer/pallas_call | solution.py:913
  160.7 6.3 %results.1 = (bf16[2,256,768]{2,1,0:T(8,128)(2,1)}, f32[512,768]{1,0:T(8,128)}, f32[576,768]{1,0:T(8,128)}, f32[192,768]{1,0:T(8,128)}, f32[768,768]{1,0:T(8,128...) custom-call(bf16[2,256,768]{2,1,0:T(8,128)(2,1)} %get-tuple-element., ...), custom_call_target="tpu_custom_call" | custom-call | tf_op jit(solution)/shard_map/results/pallas_call | solution.py:1042
